TPU v7x, 128 devices: a whole 4x4x4 slice. The times are simulated.
128 devices in a mesh: ctx: 32 (over z, y, core), ch: 4 (over x).
Axes of the slice: x: 4, y: 4, z: 4, core: 2. Of those that a mesh axis runs over, the one named last changes fastest.
Arguments:
- query: bfloat16 [4096, 4096], P('ctx', 'ch'), may hold values from -6 to 6
- key_in: bfloat16 [4096, 4096], P('ctx', 'ch'), may hold values from -6 to 6
- value_in: bfloat16 [4096, 4096], P('ctx', 'ch'), may hold values from -6 to 6
- filter_raw: bfloat16 [4096, 4096], P(None, 'ch'), may hold values from -2523.4375 to 2523.4375
- decay: float32 [4096], P('ch'), may hold values from 0.0007324219 to 0.0029296875
- skip: float32 [4096], P('ch'), may hold values from -3 to 3
- out_weight: bfloat16 [4096, 4096], P('ch'), may hold values from -0.09375 to 0.09375
- cotangent: bfloat16 [4096, 4096], P('ctx', 'ch'), may hold values from -6 to 6
Outputs:
- mixed: bfloat16 [4096, 4096], P('ctx', 'ch')
- d_query: bfloat16 [4096, 4096], P('ctx', 'ch')
- d_key: bfloat16 [4096, 4096], P('ctx', 'ch')
- d_value: bfloat16 [4096, 4096], P('ctx', 'ch')
- filter_grad: float32 [4096, 4096], P('ctx', 'ch')
- skip_grad: float32 [4096], P('ch')
All inputs are finite; a program needn't handle non-finite values.
Results may differ from a plain program's by a relative error of at most 0.013.
Values may be sent and summed in bfloat16 or wider, within the bound.
No kernel may reach another device: no remote copies, remote signals or barrier semaphores. Data moves between devices by JAX's collectives and lax.ppermute only.
A program may use at most 384 MiB of HBM per device.

v0:
```python
from functools import partial

import jax
import jax.numpy as jnp
from jax import lax
from jax.sharding import PartitionSpec as P

exact_mode = lax.Precision.HIGHEST


def transform_tables(panel_len):
    size = 2 * panel_len
    freqs = jnp.arange(panel_len, dtype=jnp.int32)
    spots = jnp.arange(size, dtype=jnp.int32)
    phase = freqs[:, None] * spots[None, :] % size
    angle = phase.astype(jnp.float32) * (2.0 * jnp.pi / size)
    parity = 1.0 - 2.0 * (spots % 2).astype(jnp.float32)
    first_mask = (freqs == 0)[:, None]
    fwd_real = jnp.cos(angle)
    fwd_imag = jnp.where(first_mask, parity[None, :], -jnp.sin(angle))
    forward = jnp.concatenate([fwd_real, fwd_imag], axis=0)
    inv_real = jnp.where(first_mask, 1.0, 2.0 * jnp.cos(angle)) / size
    inv_imag = jnp.where(first_mask, parity[None, :], -2.0 * jnp.sin(angle)) / size
    inverse = jnp.concatenate([inv_real, inv_imag], axis=0).T
    alternate = 1.0 - 2.0 * (freqs % 2).astype(jnp.float32)
    return (forward, inverse, first_mask.astype(jnp.float32), alternate)


def complex_times(left, right, first_row, panel_len):
    left_real, left_imag = (left[..., :panel_len, :], left[..., panel_len:, :])
    right_real, right_imag = (right[..., :panel_len, :], right[..., panel_len:, :])
    others = 1.0 - first_row
    real_part = left_real * right_real - others * left_imag * right_imag
    imag_part = first_row * left_imag * right_imag + others * (
        left_real * right_imag + left_imag * right_real
    )
    return jnp.concatenate([real_part, imag_part], axis=-2)


def conjugate(spectrum, first_row, panel_len):
    return jnp.concatenate(
        [spectrum[..., :panel_len, :], spectrum[..., panel_len:, :] * (2.0 * first_row - 1.0)],
        axis=-2,
    )


def signed(spectrum, alternate):
    return spectrum * jnp.concatenate([alternate, alternate])[:, None]


def add_panels(fwd_low, panel_len, carry, piece, start):
    row_count = piece.shape[0]
    values = piece.astype(jnp.float32)
    groups = row_count // panel_len
    spectrum = jnp.einsum(
        "si,pio->pso",
        fwd_low,
        values.reshape(groups, panel_len, values.shape[1]),
        precision=exact_mode,
    )
    return spectrum


def pick(stack, where):
    return lax.dynamic_index_in_dim(stack, where, 0, keepdims=False)


def local(query, key_in, value_in, filter_raw, decay, skip, out_weight, cotangent):
    panel_len = query.shape[0]
    channels = query.shape[1]
    panels = lax.axis_size("ctx")
    position = lax.axis_index("ctx")
    forward, inverse, first_row, alternate = transform_tables(panel_len)
    fwd_low = forward[:, :panel_len]
    fwd_high = forward[:, panel_len:]
    key_float = key_in.astype(jnp.float32)
    value_float = value_in.astype(jnp.float32)
    query_float = query.astype(jnp.float32)
    product_in = (key_float * value_float).astype(jnp.bfloat16)
    product_float = product_in.astype(jnp.float32)
    length = filter_raw.shape[0]
    positions = jnp.arange(length, dtype=jnp.float32)
    window = jnp.exp(-decay[None, :] * positions[:, None])
    taps = filter_raw.astype(jnp.float32) * window
    blocks = jnp.concatenate(
        [
            jnp.zeros((1, panel_len, channels), jnp.float32),
            taps.reshape(panels, panel_len, channels),
        ],
        axis=0,
    )

    def lag_spectrum(lag_index):
        lower = pick(blocks, lag_index)
        upper = pick(blocks, lag_index + 1)
        return jnp.dot(fwd_low, lower, precision=exact_mode) + jnp.dot(
            fwd_high, upper, precision=exact_mode
        )

    spectra_filter = lax.map(lag_spectrum, jnp.arange(panels, dtype=jnp.int32))
    empty = jnp.zeros((panels, 2 * panel_len, channels), jnp.float32)
    folder = partial(add_panels, fwd_low, panel_len)
    weight_cols = out_weight
    back_grad = lax.dot_general(
        lax.all_gather(cotangent, "ch", axis=1, tiled=True),
        weight_cols,
        (((1,), (1,)), ((), ())),
        preferred_element_type=jnp.float32,
    )
    conv_grad = (query_float * back_grad).astype(jnp.bfloat16)
    grad_float = conv_grad.astype(jnp.float32)
    spectra_input = folder(
        empty, lax.all_gather(product_in, "ctx", axis=0, tiled=True), jnp.int32(0)
    )
    spectra_grad = folder(empty, lax.all_gather(conv_grad, "ctx", axis=0, tiled=True), jnp.int32(0))

    def forward_term(source, running):
        lag_index = position - source
        is_valid = (lag_index >= 0).astype(jnp.float32)
        term = complex_times(
            pick(spectra_filter, jnp.maximum(lag_index, 0)),
            pick(spectra_input, source),
            first_row,
            panel_len,
        )
        return running + is_valid * term

    start_freq = jnp.zeros((2 * panel_len, channels), jnp.float32)
    conv_freq = lax.fori_loop(0, panels, forward_term, start_freq)
    convolved = (
        jnp.dot(inverse[panel_len:], conv_freq, precision=exact_mode)
        + skip[None, :] * product_float
    )
    gated = (query_float * convolved).astype(jnp.bfloat16)
    weight_cols = out_weight
    mixed = lax.psum_scatter(
        lax.dot_general(
            weight_cols, gated, (((0,), (1,)), ((), ())), preferred_element_type=jnp.float32
        ),
        "ch",
        scatter_dimension=0,
        tiled=True,
    ).T.astype(jnp.bfloat16)
    d_query = (back_grad * convolved).astype(jnp.bfloat16)

    def backward_term(target, running):
        lag_index = target - position
        is_valid = (lag_index >= 0).astype(jnp.float32)
        coeff = signed(
            conjugate(pick(spectra_filter, jnp.maximum(lag_index, 0)), first_row, panel_len),
            alternate,
        )
        return running + is_valid * complex_times(
            coeff, pick(spectra_grad, target), first_row, panel_len
        )

    back_freq = lax.fori_loop(0, panels, backward_term, start_freq)
    input_grad = (
        jnp.dot(inverse[:panel_len], back_freq, precision=exact_mode) + skip[None, :] * grad_float
    )
    d_key = (input_grad * value_float).astype(jnp.bfloat16)
    d_value = (input_grad * key_float).astype(jnp.bfloat16)

    def segment(source):
        now_spec = pick(spectra_input, jnp.maximum(source, 0))
        prev_spec = pick(spectra_input, jnp.maximum(source - 1, 0))
        has_prev = (source >= 1).astype(jnp.float32)
        return signed(now_spec, alternate) + has_prev * prev_spec

    def pair_term(target, running):
        source = target - position
        is_valid = (source >= 0).astype(jnp.float32)
        grad_spec = signed(pick(spectra_grad, target), alternate)
        pair = complex_times(
            grad_spec, conjugate(segment(source), first_row, panel_len), first_row, panel_len
        )
        return running + is_valid * pair

    pair_freq = lax.fori_loop(0, panels, pair_term, start_freq)
    lag_panel = jnp.dot(inverse[:panel_len], pair_freq, precision=exact_mode)
    own_window = lax.dynamic_slice_in_dim(window, position * panel_len, panel_len, 0)
    filter_grad = lag_panel * own_window
    skip_grad = lax.psum(jnp.sum(grad_float * product_float, axis=0), "ctx")
    return (mixed, d_query, d_key, d_value, filter_grad, skip_grad)


def solution(mesh):
    in_specs = (
        P("ctx", "ch"),
        P("ctx", "ch"),
        P("ctx", "ch"),
        P(None, "ch"),
        P("ch"),
        P("ch"),
        P("ch", None),
        P("ctx", "ch"),
    )
    out_specs = (
        P("ctx", "ch"),
        P("ctx", "ch"),
        P("ctx", "ch"),
        P("ctx", "ch"),
        P("ctx", "ch"),
        P("ch"),
    )
    return jax.shard_map(local, mesh=mesh, in_specs=in_specs, out_specs=out_specs, check_vma=False)
```

profile of v0, /device:TPU:1, one launch (start us, length us, event | category | flops | bytes accessed | tf_op | source)
XLA Modules:
  0.0 840.3 jit_solution(13664097110937386025)
XLA Ops:
  8.6 14.8 %multiply_exponential_fusion = (f32[4096,1024]{1,0:T(8,128)}, f32[4096,1024]{1,0:T(8,128)}) fusion(f32[1024]{0:T(1024)S(1)} %neg.7, bf16[4096,1024]{1,0:T(8,128)(2,1)} %param.19), kind=kLoop, calls=%fused_computation.50 | loop fusion | flops 12582912 | bytes 41947136 | tf_op jit(solution)/shard_map/exp | solution.py:83
  23.5 12.1 %concatenate.64 = f32[33,128,1024]{2,1,0:T(8,128)} pad(f32[32,128,1024]{2,1,0:T(8,128)} %bitcast.149, f32[]{:T(128)} %constant.253.clone.1), padding=1_0x0_0x0_0 | pad | bytes 34078724 | tf_op jit(solution)/shard_map/concatenate | solution.py:85
  36.9 7.6 fusion.26
  44.6 295.7 %while.61 = (s32[]{:T(128)}, f32[32,256,1024]{2,1,0:T(8,128)}, s32[32]{0:T(128)S(1)}, f32[33,128,1024]{2,1,0:T(8,128)}, f32[256,128]{1,0:T(8,128)S(1)}, /*index=...) while((s32[]{:T(128)}, f32[32,256,1024]{2,1,0:T(8,128)}, s32[32]{0:T(128)S(1)}, ...), condition=%wide.region_1.2_spmd, body=%wide.region_0.1_spmd.sunk | while | flops 805568512 | bytes 8650965 | solution.py:100
  84.0 2.1 fusion.77
  340.3 65.7 %psum.7 = f32[1024]{0:T(1024)} all-reduce(f32[1024]{0:T(1024)S(1)} %get-tuple-element.780), channel_id=1, replica_groups=mesh['ctx'=32,'ch'=4] {'ctx'}, use_global_device_ids=true, to_apply=%region_10.11 | all-reduce | flops 1024 | bytes 8192 | tf_op jit(solution)/shard_map/psum | solution.py:183
  406.3 21.4 %convolution_bitcast_fusion.1 = f32[32,256,1024]{1,2,0:T(8,128)} fusion(bf16[32,128,1024]{2,1,0:T(8,128)(2,1)} %bitcast.151, f32[256,128]{1,0:T(8,128)S(1)} %get-tuple-element.1090), kind=kOutput, calls=%fused_computation.53 | convolution fusion | flops 12884901888 | bytes 42074112 | tf_op jit(solution)/shard_map/si,pio->pso/dot_general | solution.py:55
  427.7 33.5 %copy.23 = f32[32,256,1024]{2,1,0:T(8,128)} copy(f32[32,256,1024]{1,2,0:T(8,128)} %convolution_bitcast_fusion.1) | data formatting | bytes 67108864
  461.2 70.4 %while.62 = (s32[]{:T(128)}, f32[256,1024]{1,0:T(8,128)S(1)}, s32[]{:T(128)}, f32[32,256,1024]{2,1,0:T(8,128)}, f32[32,256,1024]{2,1,0:T(8,128)}, /*index=5*/s32[]{:T(128)}, s32[]{:T(128)}, s32[]{}) while((s32[]{:T(128)}, f32[256,1024]{1,0:T(8,128)S(1)}, s32[]{:T(128)}, f32[32,256,1024]{2,1,0:T(8,128)}, ...), condition=%wide.region_3.4_spmd.clone.clone, body=%wide.region_2.3_spmd.clone.clone.sunk | while | flops 2491016 | bytes 6293673 | solution.py:129
  531.6 2.6 multiply_convert_fusion
  534.2 6.1 convolution_bitcast_fusion.2
  540.3 21.6 %convolution_bitcast_fusion = f32[32,256,1024]{1,2,0:T(8,128)} fusion(bf16[32,128,1024]{2,1,0:T(8,128)(2,1)} %bitcast.150, f32[256,128]{1,0:T(8,128)S(1)} %get-tuple-element.1090), kind=kOutput, calls=%fused_computation.52 | convolution fusion | flops 12884901888 | bytes 42074112 | tf_op jit(solution)/shard_map/si,pio->pso/dot_general | solution.py:55
  562.0 33.5 %copy.26 = f32[32,256,1024]{2,1,0:T(8,128)} copy(f32[32,256,1024]{1,2,0:T(8,128)} %convolution_bitcast_fusion) | data formatting | bytes 67108864
  595.4 138.6 %while.63 = (s32[]{:T(128)}, f32[256,1024]{1,0:T(8,128)S(1)}, s32[]{:T(128)}, f32[32,256,1024]{2,1,0:T(8,128)}, f32[256]{0:T(256)S(1)}, /*index=5*/f32[32,256,1024]{2,1,0:T(8,128)}, s32[]{:T(128)}, s32[]{:T(128)}, s32[]{}) while((s32[]{:T(128)}, f32[256,1024]{1,0:T(8,128)S(1)}, s32[]{:T(128)}, ...), condition=%wide.region_6.7_spmd.clone.clone, body=%wide.region_5.6_spmd.clone.clone.sunk | while | flops 3146632 | bytes 10490041 | solution.py:157
  734.0 92.6 %while.64 = (s32[]{:T(128)}, f32[256,1024]{1,0:T(8,128)S(1)}, s32[]{:T(128)}, f32[32,256,1024]{2,1,0:T(8,128)}, f32[256]{0:T(256)S(1)}, /*index=5*/f32[32,256,1024]{2,1,0:T(8,128)}, s32[]{:T(128)}, s32[]{:T(128)}, s32[]{:T(128)}) while((s32[]{:T(128)}, f32[256,1024]{1,0:T(8,128)S(1)}, s32[]{:T(128)}, ...), condition=%wide.region_8.9_spmd.clone.clone, body=%wide.region_7.8_spmd.clone.clone.sunk | while | flops 3670923 | bytes 11538639 | solution.py:179
  734.1 2.1 bitcast_add_fusion.2
  739.9 2.1 bitcast_add_fusion.2
  742.8 2.1 bitcast_add_fusion.2
  745.7 2.1 bitcast_add_fusion.2
  748.6 2.1 bitcast_add_fusion.2
  754.4 2.1 bitcast_add_fusion.2
  815.1 2.1 bitcast_add_fusion.2
  826.7 2.6 convolution_multiply_fusion
  829.3 2.7 fusion.23
  (706 shorter events, 479.0 us)
Async XLA Ops:
  7.2 29.8 %all-gather.6.cloned.1.call-start = ((), (), s32[]{:S(2)}) async-start(), calls=%async_computation.3 | async-start | bytes 1310720 | tf_op jit(solution)/shard_map/all_gather | solution.py:105
  7.9 398.4 %all-gather.4.cloned.1.call-start = ((), (), s32[]{:S(2)}) async-start(), calls=%async_computation.1 | async-start | bytes 8650752 | tf_op jit(solution)/shard_map/all_gather | solution.py:113
  23.5 13.5 %copy-start.4 = (bf16[128,1024]{1,0:T(8,128)(2,1)S(1)}, bf16[128,1024]{1,0:T(8,128)(2,1)}, u32[]{:S(2)}) copy-start(bf16[128,1024]{1,0:T(8,128)(2,1)} %param.16) | copy-start | bytes 786436
  23.5 13.5 %copy-start.5 = (bf16[128,1024]{1,0:T(8,128)(2,1)S(1)}, bf16[128,1024]{1,0:T(8,128)(2,1)}, u32[]{:S(2)}) copy-start(bf16[128,1024]{1,0:T(8,128)(2,1)} %param.18) | copy-start | bytes 786436
  23.5 13.4 %copy-start.6 = (bf16[128,1024]{1,0:T(8,128)(2,1)S(1)}, bf16[128,1024]{1,0:T(8,128)(2,1)}, u32[]{:S(2)}) copy-start(bf16[128,1024]{1,0:T(8,128)(2,1)} %param.17) | copy-start | bytes 786436
  44.6 495.7 %all-gather.8.cloned.1.call-start = ((), (), s32[]{:S(2)}) async-start(), calls=%async_computation.4 | async-start | bytes 8650752 | tf_op jit(solution)/shard_map/all_gather | solution.py:115
  406.0 425.9 %reduce-scatter.2.cloned.1.call-start = ((), (), s32[]{:S(2)}) async-start(), calls=%async_computation.2 | async-start | bytes 2621440 | tf_op jit(solution)/shard_map/reduce_scatter | solution.py:136
  427.7 33.5 %copy-start.1 = (f32[256,1024]{1,0:T(8,128)S(1)}, f32[256,1024]{1,0:T(8,128)}, u32[]{:S(2)}) copy-start(f32[256,1024]{1,0:T(8,128)} %custom-call) | copy-start | bytes 3145732
  461.2 70.4 %copy-start.3 = (bf16[128,1024]{1,0:T(8,128)(2,1)S(1)}, bf16[128,1024]{1,0:T(8,128)(2,1)}, u32[]{:S(2)}) copy-start(bf16[128,1024]{1,0:T(8,128)(2,1)} %get-tuple-element.782) | copy-start | bytes 786436
  461.2 70.4 %copy-start.7 = (f32[1024]{0:T(1024)S(1)}, f32[1024]{0:T(1024)}, u32[]{:S(2)}) copy-start(f32[1024]{0:T(1024)} %param.21) | copy-start | bytes 12292
  562.0 33.5 %copy-start = (f32[256,1024]{1,0:T(8,128)S(1)}, f32[256,1024]{1,0:T(8,128)}, u32[]{:S(2)}) copy-start(f32[256,1024]{1,0:T(8,128)} %custom-call.1) | copy-start | bytes 3145732
  734.0 95.3 %copy-start.2 = (bf16[128,1024]{1,0:T(8,128)(2,1)S(1)}, bf16[128,1024]{1,0:T(8,128)(2,1)}, u32[]{:S(2)}) copy-start(bf16[128,1024]{1,0:T(8,128)(2,1)} %get-tuple-element.781) | copy-start | bytes 786436
Sparse Core Ops, SparseCore 0:
  9.7 26.2 all-gather.5
  44.7 56.7 all-gather.3
  406.1 54.1 all-gather.7
  540.4 30.5 reduce-scatter.1
where the time goes:
time: 855 us; the launch traced here: 840 us
  other arithmetic  279 us (33%)
  matrix products  197 us (23%)
  local copies, waits for them, and re-layouts  177 us (21%)
  loops' own time  106 us (12%)
  blocking collectives  65.7 us (8%)
  between operations  13.9 us (2%)
    sub x96, other arithmetic, complex_times(): real_part = left_real * right_real - others * left_imag * right_imag  116 us
    another operation x1, loops' own time, local(): spectra_filter = lax.map(lag_spectrum, jnp.arange(panels, dtype=jnp.int32))  99.8 us
    add x32, other arithmetic, segment(): return signed(now_spec, alternate) + has_prev * prev_spec  67.1 us
    unnamed x18, local copies, waits for them, and re-layouts  67 us
    dot_general x32, matrix products, lag_spectrum(): jnp.dot(fwd_low, lower, precision=exact_mode)  66.1 us
    dot_general x32, matrix products, lag_spectrum(): jnp.dot(fwd_high, upper, precision=exact_mode)  66.1 us
    psum x1, blocking collectives, local(): skip_grad = lax.psum(jnp.sum(grad_float * product_float, axis=0), 'ctx')  65.7 us
    dynamic_update_slice x64, local copies, waits for them, and re-layouts, local(): spectra_filter = lax.map(lag_spectrum, jnp.arange(panels, dtype=jnp.int32))  44.8 us
  transfers between devices with their start and end apart: 4, of which 0 were waited for; matrix products, arithmetic and copies ran while one was open for 77% of the time, Pallas kernels for 0%

commit v1 on v0

v1 whole, which is shorter than its diff:
```python
from functools import partial

import jax
import jax.numpy as jnp
import ml_dtypes
import numpy as np
from jax import lax
from jax.experimental import pallas as pl
from jax.experimental.pallas import tpu as pltpu
from jax.sharding import PartitionSpec as P

PANEL = 128
PANELS = 32
OWN = 32
CHB = 1024
ROWS = PANELS * OWN
SPLIT = 4
PAIRS = OWN // 2
TAIL = 16
GROUP = 8
F32 = jnp.float32
BF16 = jnp.bfloat16
LIMIT = 24 * 1024 * 1024


def tables():
    freq = np.arange(PANEL) + 0.5
    spot = np.arange(PANEL)
    angle = 2 * np.pi * spot[:, None] * freq[None, :] / (2 * PANEL)
    inner = np.concatenate([np.cos(angle), -np.sin(angle)], axis=1)
    inner_back = np.concatenate([np.cos(angle.T), -np.sin(angle.T)], axis=0) / (
        PANEL * 2 * PANELS
    )
    turn = 2 * np.pi * np.arange(2 * PANELS)[:, None] * np.arange(PANELS)[None, :] / (2 * PANELS)
    cos, sin = np.cos(turn), np.sin(turn)
    outer = np.concatenate(
        [np.concatenate([cos, sin], axis=1), np.concatenate([-sin, cos], axis=1)], axis=0
    )
    outer_back = np.concatenate(
        [np.concatenate([cos.T, -sin.T], axis=1), np.concatenate([sin.T, cos.T], axis=1)], axis=0
    )
    return [m.astype(ml_dtypes.bfloat16) for m in (inner, outer, outer_back, inner_back)]


def dot(left, right):
    return jnp.dot(left, right, preferred_element_type=F32)


def dot_rows(left, right):
    return lax.dot_general(left, right, (((1,), (1,)), ((), ())), preferred_element_type=F32)


def spectrum(load, inner, outer, mid_ref, store):
    step = 8
    for a in range(0, PANELS, step):
        rows = dot(jnp.concatenate([load(a + b) for b in range(step)], axis=0), inner)
        mid_ref[0, pl.ds(a * OWN, step * OWN), :] = rows[:, :PANEL]
        mid_ref[1, pl.ds(a * OWN, step * OWN), :] = rows[:, PANEL:]
    for pair in range(PAIRS):
        quarter = [
            [mid_ref[part, pl.ds(2 * pair + c, PANELS, stride=OWN), :].astype(BF16) for c in (0, 1)]
            for part in (0, 1)
        ]
        both = jnp.concatenate([jnp.concatenate(q, axis=1) for q in quarter], axis=0)
        store(pair, dot(outer, both))


def spread(pair, freq, outer_back, mid_ref):
    back = dot(outer_back, freq.astype(BF16))
    for part in (0, 1):
        for c in (0, 1):
            mid_ref[part, pl.ds(2 * pair + c, PANELS, stride=OWN), :] = back[
                part * PANELS : (part + 1) * PANELS, c * PANEL : (c + 1) * PANEL
            ]


def gather_panels(mid_ref, inner_back, shift, store):
    lanes = lax.broadcasted_iota(jnp.int32, (1, PANEL), 1)
    sign = (1.0 - 2.0 * (lanes % 2).astype(F32)) * shift
    step = 8
    for a in range(0, PANELS, step):
        parts = []
        for b in range(a, a + step):
            real = mid_ref[0, pl.ds(b * OWN, OWN), :]
            imag = mid_ref[1, pl.ds(b * OWN, OWN), :]
            other = b - shift
            if 0 <= other < PANELS:
                there_real = mid_ref[0, pl.ds(other * OWN, OWN), :]
                there_imag = mid_ref[1, pl.ds(other * OWN, OWN), :]
                real = real - sign * there_imag
                imag = imag + sign * there_real
            parts.append(jnp.concatenate([real.astype(BF16), imag.astype(BF16)], axis=1))
        done = dot(jnp.concatenate(parts, axis=0), inner_back)
        for b in range(step):
            store(a + b, done[b * OWN : (b + 1) * OWN])


def product_kernel(key_ref, value_ref, out_ref, key_held, value_held, sems):
    copies = [
        pltpu.make_async_copy(ref, held, sems.at[n])
        for n, (ref, held) in enumerate(((key_ref, key_held), (value_ref, value_held)))
    ]
    for copy in copies:
        copy.start()
    for copy in copies:
        copy.wait()
    product = key_held[...].astype(F32) * value_held[...].astype(F32)
    out_ref[...] = product.T.astype(BF16).reshape(PANELS, OWN, PANEL)


def filter_kernel(
    where_ref,
    raw_ref,
    decay_ref,
    inner_from,
    outer_from,
    freq_to,
    rate_ref,
    inner_ref,
    outer_ref,
    freq_ref,
    raw_held,
    decay_held,
    taps_ref,
    mid_ref,
    sems,
):
    column = pl.multiple_of(lax.div(where_ref[0], SPLIT) * PANEL, PANEL)
    moves = (
        (raw_ref.at[:, pl.ds(column, PANEL)], raw_held),
        (decay_ref, decay_held),
        (inner_from, inner_ref),
        (outer_from, outer_ref),
    )
    copies = [pltpu.make_async_copy(here, there, sems.at[n]) for n, (here, there) in enumerate(moves)]
    for copy in copies:
        copy.start()
    for copy in copies:
        copy.wait()
    place = lax.rem(where_ref[0], SPLIT) * OWN
    row = lax.broadcasted_iota(jnp.int32, (OWN, PANEL), 0)
    lane = lax.broadcasted_iota(jnp.int32, (OWN, PANEL), 1)
    mine = lane == row + place
    rates = decay_held[pl.ds(lax.div(where_ref[0], SPLIT), 1), :]
    rate = jnp.sum(jnp.where(mine, rates, 0.0), axis=1, keepdims=True)
    rate = jnp.broadcast_to(rate, (OWN, PANEL))
    rate_ref[...] = rate
    choose = mine.astype(BF16)
    step = 4
    for a in range(0, PANELS, step):
        chosen = dot_rows(choose, raw_held[pl.ds(a * PANEL, step * PANEL), :])
        for b in range(step):
            spot = (lane + (a + b) * PANEL).astype(F32)
            taps = chosen[:, b * PANEL : (b + 1) * PANEL] * jnp.exp(-rate * spot)
            taps_ref[a + b] = taps.astype(BF16)

    group = 4
    writes = []

    def store(pair, value):
        freq_ref[pair] = value
        if (pair + 1) % group == 0:
            part = pl.ds(pair + 1 - group, group)
            copy = pltpu.make_async_copy(
                freq_ref.at[part], freq_to.at[part], sems.at[4 + pair // group]
            )
            copy.start()
            writes.append(copy)

    spectrum(lambda a: taps_ref[a], inner_ref[...], outer_ref[...], mid_ref, store)
    for copy in writes:
        copy.wait()


def halves(value):
    return value[: 2 * PANELS], value[2 * PANELS :]


def forward_kernel(
    where_ref,
    x_ref,
    filter_from,
    inner_ref,
    outer_ref,
    outer_back_from,
    inner_back_from,
    query_ref,
    cot0_ref,
    cot1_ref,
    cot2_ref,
    cot3_ref,
    weight_ref,
    send_ref,
    freq_ref,
    back_ref,
    grad_ref,
    mid_ref,
    out_mid_ref,
    outer_back_ref,
    inner_back_ref,
    filter_ref,
    cot_held,
    weight_held,
    sems,
):
    moves = [
        (outer_back_from, outer_back_ref),
        (inner_back_from, inner_back_ref),
        (filter_from, filter_ref),
    ]
    for s, cot_ref in enumerate((cot0_ref, cot1_ref, cot2_ref, cot3_ref)):
        block = lax.rem(where_ref[1] + SPLIT - s, SPLIT)
        columns = pl.ds(pl.multiple_of(block * CHB, CHB), CHB)
        moves += [(cot_ref, cot_held.at[s]), (weight_ref.at[:, columns], weight_held.at[s])]
    copies = [pltpu.make_async_copy(there, to, sems.at[n]) for n, (there, to) in enumerate(moves)]
    for copy in copies:
        copy.start()

    def store(pair, value):
        freq_ref[pair] = value

    spectrum(lambda a: x_ref[a], inner_ref[...], outer_ref[...], mid_ref, store)
    for copy in copies[:3]:
        copy.wait()
    outer_back = outer_back_ref[...]
    for pair in range(PAIRS):
        xr, xi = halves(freq_ref[pair])
        hr, hi = halves(filter_ref[pair])
        spread(
            pair,
            jnp.concatenate([hr * xr - hi * xi, hr * xi + hi * xr], axis=0),
            outer_back,
            out_mid_ref,
        )

    def store_panel(a, value):
        send_ref[a, :OWN, :] = value.astype(BF16)

    gather_panels(out_mid_ref, inner_back_ref[...], 1, store_panel)
    for copy in copies[3:]:
        copy.wait()
    chunk = 256
    for c in range(0, CHB, chunk):
        total = jnp.zeros((PANEL, chunk), F32)
        for s in range(SPLIT):
            total += dot_rows(cot_held[s], weight_held[s, pl.ds(c, chunk), :])
        back_ref[:, pl.ds(c, chunk)] = total
        grad = query_ref[:, pl.ds(c, chunk)].astype(F32) * total
        grad_ref[:, pl.ds(c, chunk)] = grad.astype(BF16)
        turned = grad.T.astype(BF16)
        for b in range(chunk // OWN):
            send_ref[c // OWN + b, OWN:, :] = turned[b * OWN : (b + 1) * OWN]


def middle_kernel(
    where_ref,
    got_ref,
    x_ref,
    freq_ref,
    rate_ref,
    inner_ref,
    outer_ref,
    query_ref,
    key_ref,
    value_ref,
    skip_ref,
    back_ref,
    filter_from,
    outer_back_from,
    inner_back_from,
    weight_from,
    own_to,
    one_to,
    two_to,
    three_to,
    send_to,
    d_query_ref,
    outer_back_ref,
    inner_back_ref,
    filter_ref,
    weight_ref,
    spec_ref,
    mid_ref,
    lag_mid_ref,
    in_mid_ref,
    gated_ref,
    own_ref,
    part_ref,
    send_ref,
    sems,
):
    order = (2, 1, 3, 0)
    moves = [
        (outer_back_from, outer_back_ref),
        (inner_back_from, inner_back_ref),
        (filter_from, filter_ref),
    ]
    for s in order:
        block = lax.rem(where_ref[1] + s, SPLIT)
        columns = pl.ds(pl.multiple_of(block * CHB, CHB), CHB)
        moves.append((weight_from.at[:, columns], weight_ref.at[s]))
    loads = [pltpu.make_async_copy(there, to, sems.at[n]) for n, (there, to) in enumerate(moves)]
    for copy in loads:
        copy.start()
    writes = []

    def write(there, to):
        copy = pltpu.make_async_copy(there, to, sems.at[len(loads) + len(writes)])
        copy.start()
        writes.append(copy)

    def store(pair, value):
        spec_ref[pair] = value

    spectrum(lambda a: got_ref[a, OWN:, :], inner_ref[...], outer_ref[...], mid_ref, store)
    for copy in loads[:3]:
        copy.wait()
    outer_back = outer_back_ref[...]
    for pair in range(PAIRS):
        gr, gi = halves(spec_ref[pair])
        for other_ref, out_ref in ((filter_ref, in_mid_ref), (freq_ref, lag_mid_ref)):
            hr, hi = halves(other_ref[pair])
            spread(
                pair,
                jnp.concatenate([gr * hr + gi * hi, gi * hr - gr * hi], axis=0),
                outer_back,
                out_ref,
            )

    chunk = 256
    for c in range(0, CHB, chunk):
        at = pl.ds(c, chunk)
        turned = got_ref[pl.ds(c // OWN, chunk // OWN), :OWN, :].reshape(chunk, PANEL).astype(F32).T
        product = (key_ref[:, at].astype(F32) * value_ref[:, at].astype(F32)).astype(BF16)
        convolved = turned + skip_ref[:, at] * product.astype(F32)
        gated_ref[:, at] = (query_ref[:, at].astype(F32) * convolved).astype(BF16)
        d_query_ref[:, at] = (back_ref[:, at] * convolved).astype(BF16)
    outs = (own_to, one_to, two_to, three_to)
    for n, s in enumerate(order):
        loads[3 + n].wait()
        for c in range(0, CHB, chunk):
            part = dot(gated_ref[...], weight_ref[s, :, pl.ds(c, chunk)])
            if s:
                part_ref[s - 1, :, pl.ds(c, chunk)] = part.astype(BF16)
            else:
                own_ref[:, pl.ds(c, chunk)] = part
        write(part_ref.at[s - 1] if s else own_ref, outs[s])

    def store_input(a, value):
        send_ref[a, :OWN, :] = value.astype(BF16)

    gather_panels(in_mid_ref, inner_back_ref[...], -1, store_input)
    rate = rate_ref[...]
    lane = lax.broadcasted_iota(jnp.int32, (OWN, PANEL), 1)
    sums = jnp.zeros((OWN, PANEL), F32)
    for a in range(PANELS):
        sums += got_ref[a, OWN:, :].astype(F32) * x_ref[a].astype(F32)
    total = jnp.sum(sums, axis=1, keepdims=True)
    place = lax.rem(where_ref[0], SPLIT) * OWN
    row = lax.broadcasted_iota(jnp.int32, (OWN, PANEL), 0)
    line = jnp.sum(jnp.where(lane == row + place, total, 0.0), axis=0, keepdims=True)
    high = line.astype(BF16).astype(F32)
    low = line - high
    index = lax.broadcasted_iota(jnp.int32, (TAIL, PANEL), 0)
    tail = jnp.where(index == 0, high, jnp.where(index == 1, low, 0.0)).astype(BF16)
    for a in range(PANELS):
        send_ref[a, 2 * OWN :, :] = tail

    def store_lag(a, value):
        window = jnp.exp(-rate * (lane + a * PANEL).astype(F32))
        send_ref[a, OWN : 2 * OWN, :] = (value * window).astype(BF16)
        if (a + 1) % GROUP == 0:
            part = pl.ds(a + 1 - GROUP, GROUP)
            write(send_ref.at[part], send_to.at[part])

    gather_panels(lag_mid_ref, inner_back_ref[...], -1, store_lag)
    for copy in writes:
        copy.wait()


def mixed_kernel(own_from, one_ref, two_ref, three_ref, mixed_ref, own_ref, sem):
    copy = pltpu.make_async_copy(own_from, own_ref, sem)
    copy.start()
    copy.wait()
    chunk = 256
    for c in range(0, CHB, chunk):
        at = pl.ds(c, chunk)
        mixed = own_ref[:, at] + one_ref[:, at].astype(F32)
        mixed += two_ref[:, at].astype(F32) + three_ref[:, at].astype(F32)
        mixed_ref[:, at] = mixed.astype(BF16)


def finish_kernel(
    got_ref,
    key_ref,
    value_ref,
    grad_ref,
    skip_ref,
    d_key_ref,
    d_value_ref,
    lag_ref,
    skip_grad_ref,
):
    chunk = 256
    for c in range(0, CHB, chunk):
        at = pl.ds(c, chunk)
        block = pl.ds(c // OWN, chunk // OWN)
        lag_ref[:, at] = got_ref[block, OWN : 2 * OWN, :].reshape(chunk, PANEL).astype(F32).T
        turned = got_ref[block, :OWN, :].reshape(chunk, PANEL).astype(F32).T
        grad = turned + skip_ref[:, at] * grad_ref[:, at].astype(F32)
        d_key_ref[:, at] = (grad * value_ref[:, at].astype(F32)).astype(BF16)
        d_value_ref[:, at] = (grad * key_ref[:, at].astype(F32)).astype(BF16)
    for r in range(PANELS // SPLIT):
        line = jnp.zeros((1, PANEL), F32)
        for b in range(SPLIT):
            tail = got_ref[r * SPLIT + b, 2 * OWN :, :].astype(F32)
            line += tail[0:1] + tail[1:2]
        skip_grad_ref[pl.ds(r, 1), :] = line


VMEM = pl.BlockSpec(memory_space=pltpu.VMEM)
SMEM = pl.BlockSpec(memory_space=pltpu.SMEM)
HBM = pl.BlockSpec(memory_space=pltpu.HBM)
ANY = pl.BlockSpec(memory_space=pl.ANY)
FREQ = (PAIRS, 4 * PANELS, 2 * PANEL)
MID = pltpu.VMEM((2, ROWS, PANEL), F32)
BLOCK = (PANEL, CHB)


def shape(dims, kind):
    return jax.ShapeDtypeStruct(dims, kind)


def here(dims, kind):
    return pltpu.VMEM(dims, kind)


def far(dims, kind):
    return pltpu.HBM(dims, kind)


def call(kernel, in_specs, out_shape, scratch, flops, name, out_specs=None):
    run = pl.pallas_call(
        kernel,
        in_specs=in_specs,
        out_specs=out_specs or jax.tree.map(lambda _: VMEM, out_shape),
        out_shape=out_shape,
        scratch_shapes=scratch,
        compiler_params=pltpu.CompilerParams(vmem_limit_bytes=LIMIT),
        cost_estimate=pl.CostEstimate(flops=flops, bytes_accessed=1 << 20, transcendentals=0),
        name=name,
    )

    def bound(*args):
        return run(
            *(
                pltpu.with_memory_space_constraint(arg, pltpu.HBM) if spec is HBM else arg
                for arg, spec in zip(args, in_specs, strict=True)
            )
        )

    return bound


def make_product(key_in, value_in):
    scratch = [pltpu.VMEM(BLOCK, BF16), pltpu.VMEM(BLOCK, BF16), pltpu.SemaphoreType.DMA((2,))]
    return call(
        product_kernel, [HBM] * 2, shape((PANELS, OWN, PANEL), BF16), scratch, 1 << 20, "product"
    )(key_in, value_in)


def make_filter(where, filter_raw, decay, inner, outer):
    out = [far(FREQ, F32), here((OWN, PANEL), F32)]
    out += [here(m.shape, BF16) for m in (inner, outer)]
    scratch = [
        pltpu.VMEM(FREQ, F32),
        pltpu.VMEM((PANELS * PANEL, PANEL), BF16),
        pltpu.VMEM(decay.shape, F32),
        pltpu.VMEM((PANELS, OWN, PANEL), BF16),
        MID,
        pltpu.SemaphoreType.DMA((8,)),
    ]
    specs = [SMEM] + [HBM] * 4
    return call(filter_kernel, specs, out, scratch, 1 << 32, "taps", [HBM] + [VMEM] * 3)(
        where, filter_raw, decay, inner, outer
    )


def make_forward(where, x, freq_filter, mats, query, cots, weight):
    out = [
        shape((PANELS, 2 * OWN, PANEL), BF16),
        here(FREQ, F32),
        here(BLOCK, F32),
        here(BLOCK, BF16),
    ]
    scratch = [
        MID,
        MID,
        pltpu.VMEM(mats[2].shape, BF16),
        pltpu.VMEM(mats[3].shape, BF16),
        pltpu.VMEM(FREQ, F32),
        pltpu.VMEM((SPLIT, *BLOCK), BF16),
        pltpu.VMEM((SPLIT, CHB, CHB), BF16),
        pltpu.SemaphoreType.DMA((3 + 2 * SPLIT,)),
    ]
    specs = [SMEM, VMEM, HBM, VMEM, VMEM] + [HBM] * 2 + [VMEM, HBM] + [ANY] * 3 + [HBM]
    return call(
        forward_kernel, specs, out, scratch, 1 << 33, "forward"
    )(where, x, freq_filter, *mats, query, *cots, weight)


def make_middle(where, got, x, freq_x, rate, held, query, key_in, value_in, skip, back, *rest):
    dims = (PANELS, 2 * OWN + TAIL, PANEL)
    out = [far(BLOCK, F32)] + [far(BLOCK, BF16)] * 3 + [far(dims, BF16), shape(BLOCK, BF16)]
    scratch = [
        pltpu.VMEM(rest[1].shape, BF16),
        pltpu.VMEM(rest[2].shape, BF16),
        pltpu.VMEM(FREQ, F32),
        pltpu.VMEM((SPLIT, CHB, CHB), BF16),
        pltpu.VMEM(FREQ, F32),
        MID,
        MID,
        MID,
        pltpu.VMEM(BLOCK, BF16),
        pltpu.VMEM(BLOCK, F32),
        pltpu.VMEM((SPLIT - 1, *BLOCK), BF16),
        pltpu.VMEM(dims, BF16),
        pltpu.SemaphoreType.DMA((3 + 2 * SPLIT + PANELS // GROUP,)),
    ]
    return call(
        middle_kernel,
        [SMEM] + [VMEM] * 11 + [HBM] * 4,
        out,
        scratch,
        1 << 33,
        "middle",
        [HBM] * 5 + [VMEM],
    )(where, got, x, freq_x, rate, *held, query, key_in, value_in, skip, back, *rest)


def make_mixed(parts):
    scratch = [pltpu.VMEM(BLOCK, F32), pltpu.SemaphoreType.DMA]
    specs = [HBM] + [VMEM] * 3
    return call(mixed_kernel, specs, shape(BLOCK, BF16), scratch, 1 << 36, "mixed")(*parts)


def make_finish(got, key_in, value_in, grad, skip):
    out = [shape(BLOCK, BF16)] * 2 + [shape(BLOCK, F32), shape((CHB // PANEL, PANEL), F32)]
    return call(finish_kernel, [VMEM] * 5, out, [], 1 << 20, "finish")(
        got, key_in, value_in, grad, skip
    )


def shifted(value, step):
    return lax.ppermute(value, "ch", [(i, (i + step) % SPLIT) for i in range(SPLIT)])


def exchange(value):
    return lax.all_to_all(value, "ctx", 0, 0)


def local(query, key_in, value_in, filter_raw, decay, skip, out_weight, cotangent):
    mats = [jnp.asarray(m) for m in tables()]
    where = jnp.stack([lax.axis_index("ctx"), lax.axis_index("ch")]).astype(jnp.int32)
    cots = [cotangent] + [shifted(cotangent, s) for s in (1, 2, 3)]
    x = exchange(make_product(key_in, value_in))
    freq_filter, rate, *held = make_filter(
        where, filter_raw, decay.reshape(CHB // PANEL, PANEL), *mats[:2]
    )
    send, freq_x, back, grad = make_forward(
        where, x, freq_filter, held + mats[2:], query, cots, out_weight
    )
    got = exchange(send)
    skip_row = skip.reshape(1, CHB)
    rest = (freq_filter, *mats[2:], out_weight)
    own, one, two, three, last, d_query = make_middle(
        where, got, x, freq_x, rate, held, query, key_in, value_in, skip_row, back, *rest
    )
    last = exchange(last)
    mixed = make_mixed([own, shifted(one, 1), shifted(two, 2), shifted(three, 3)])
    d_key, d_value, filter_grad, skip_grad = make_finish(last, key_in, value_in, grad, skip_row)
    return (mixed, d_query, d_key, d_value, filter_grad, skip_grad.reshape(CHB))


def solution(mesh):
    in_specs = (
        P("ctx", "ch"),
        P("ctx", "ch"),
        P("ctx", "ch"),
        P(None, "ch"),
        P("ch"),
        P("ch"),
        P("ch", None),
        P("ctx", "ch"),
    )
    out_specs = (
        P("ctx", "ch"),
        P("ctx", "ch"),
        P("ctx", "ch"),
        P("ctx", "ch"),
        P("ctx", "ch"),
        P("ch"),
    )
    return jax.shard_map(local, mesh=mesh, in_specs=in_specs, out_specs=out_specs, check_vma=False)
```

time: 855 us -> 81.7 us (0.10); the launches traced: 840 us -> 81.3 us
  other arithmetic: 279 us -> 0.08 us
  matrix products: 197 us -> 0 us
  local copies, waits for them, and re-layouts: 177 us -> 0.03 us
  loops' own time: 106 us -> 0 us
  blocking collectives: 65.7 us -> 15.1 us
  Pallas kernels: 0 us -> 26.4 us
  starting transfers between devices: 0.34 us -> 23.4 us
  waiting for transfers between devices: 0.77 us -> 15.5 us
  between operations: 13.9 us -> 0.75 us
    dot_general x71 -> x0, matrix products: 197 us -> none  [the longest x32 66.1 us: lag_spectrum(): jnp.dot(fwd_low, lower, precision=exact_mode)]
    sub x194 -> x0, other arithmetic: 116 us -> none  [the longest x96 116 us: complex_times(): real_part = left_real * right_real - others * left_imag * right_imag]
    another operation x4 -> x0, loops' own time: 106 us -> none  [the longest x1 99.8 us: local(): spectra_filter = lax.map(lag_spectrum, jnp.arange(panels, dtype=jnp.int32))]
    add x128 -> x0, other arithmetic: 102 us -> none  [the longest x32 67.1 us: segment(): return signed(now_spec, alternate) + has_prev * prev_spec]
    unnamed x18 -> x8, local copies, waits for them, and re-layouts: 67 us -> 0.03 us
    psum x1 -> x0, blocking collectives: 65.7 us -> none  [local(): skip_grad = lax.psum(jnp.sum(grad_float * product_float, axis=0), 'ctx')]
    dynamic_update_slice x64 -> x0, local copies, waits for them, and re-layouts: 44.8 us -> none  [local(): spectra_filter = lax.map(lag_spectrum, jnp.arange(panels, dtype=jnp.int32))]
    mul x64 -> x0, other arithmetic: 41.1 us -> none  [the longest x32 36.8 us: conjugate(): spectrum[..., panel_len:, :] * (2.0 * first_row - 1.0)]
  transfers between devices with their start and end apart: 4 -> 8, of which waited for: 0 -> 4; matrix products, arithmetic and copies ran while one was open for 77% -> 0% of each run, Pallas kernels for 0% -> 10%
where the time goes in v1:
time: 81.7 us; the launch traced here: 81.3 us
  Pallas kernels  26.4 us (32%)
  starting transfers between devices  23.4 us (29%)
  waiting for transfers between devices  15.5 us (19%)
  blocking collectives  15.1 us (18%)
    pallas_call x6, Pallas kernels, bound(): run(*(pltpu.with_memory_space_constraint(arg, pltpu.HBM) if spec is HBM e...  26.4 us
    all_to_all x1, blocking collectives, exchange(): return lax.all_to_all(value, 'ctx', 0, 0)  15.1 us
    all_to_all x2, starting transfers between devices, exchange(): return lax.all_to_all(value, 'ctx', 0, 0)  14.3 us
    ppermute x6, starting transfers between devices, shifted(): lax.ppermute(value, 'ch', [(i, (i + step) % SPLIT) for i in range(SPLIT)])  9.07 us
    all_to_all x2, waiting for transfers between devices, exchange(): return lax.all_to_all(value, 'ctx', 0, 0)  7.9 us
    ppermute x6, waiting for transfers between devices, shifted(): lax.ppermute(value, 'ch', [(i, (i + step) % SPLIT) for i in range(SPLIT)])  7.58 us
  transfers between devices with their start and end apart: 8, of which 4 were waited for; matrix products, arithmetic and copies ran while one was open for 0% of the time, Pallas kernels for 10%

profile of v1, /device:TPU:1, one launch (start us, length us, event | category | flops | bytes accessed | tf_op | source)
XLA Modules:
  0.0 81.3 jit_solution(12743644969669761008)
XLA Ops:
  0.6 3.7 %collective-permute-start.1 = (bf16[128,1024]{1,0:T(8,128)(2,1)}, bf16[128,1024]{1,0:T(8,128)(2,1)S(1)}, u32[]{:S(2)}, u32[]{:S(2)}) collective-permute-start(bf16[128,1024]{1,0:T(8,128)(2,1)} %cot0_ref.1), channel_id=1, source_target_pairs={{0,2},{1,3},{2,0},{3,1},{4,6},{5,7},{6,4},{7,5},{8,10},{9,11},{10,... | collective-permute-start | bytes 786440 | tf_op jit(solution)/shard_map/ppermute | solution.py:555
  4.3 0.3 collective-permute-start
  4.6 2.4 %collective-permute-start.2 = (bf16[128,1024]{1,0:T(8,128)(2,1)}, bf16[128,1024]{1,0:T(8,128)(2,1)S(1)}, u32[]{:S(2)}, u32[]{:S(2)}) collective-permute-start(bf16[128,1024]{1,0:T(8,128)(2,1)} %cot0_ref.1), channel_id=1, source_target_pairs={{0,3},{1,0},{2,1},{3,2},{4,7},{5,4},{6,5},{7,6},{8,11},{9,8},{10,9... | collective-permute-start | bytes 786440 | tf_op jit(solution)/shard_map/ppermute | solution.py:555
  7.0 1.9 %product.1 = bf16[32,32,128]{2,1,0:T(8,128)(2,1)} custom-call(bf16[128,1024]{1,0:T(8,128)(2,1)} %key_ref.5, bf16[128,1024]{1,0:T(8,128)(2,1)} %value_ref.5), custom_call_target="tpu_custom_call" | custom-call | flops 1048576 | bytes 1048576 | tf_op jit(solution)/shard_map/product/pallas_call | solution.py:455
  8.9 0.0 copy-start.3
  8.9 9.8 %all-to-all-start = ((bf16[32,32,128]{2,1,0:T(8,128)(2,1)}), bf16[32,32,128]{2,1,0:T(8,128)(2,1)S(1)}, u32[]{:S(2)}, u32[]{:S(2)}) async-start(bf16[32,32,128]{2,1,0:T(8,128)(2,1)} %product.1), calls=%async_computation | async-start | bytes 524288 | tf_op jit(solution)/shard_map/all_to_all | solution.py:559
  18.6 0.1 pad_add_fusion.where_ref
  18.7 4.5 %taps.1 = (f32[16,128,256]{2,1,0:T(8,128)}, f32[32,128]{1,0:T(8,128)S(1)}, bf16[128,256]{1,0:T(8,128)(2,1)S(1)}, bf16[128,64]{1,0:T(8,128)(2,1)S(1)}) custom-call(s32[2]{0:T(128)S(1)} %pad_add_fusion.where_ref, bf16[4096,1024]{1,0:T(8,128)(2,1)} %raw_ref.1, f32[8,128]{1,0:T(8,128)} %bitcast.7, bf16[128,256]{1,0:T(8,128)(2,1)} %constant.17.clone.inner_from, ...), custom_call_target="tpu_custom_call" | custom-call | flops 4294967296 | bytes 1048576 | tf_op jit(solution)/shard_map/taps/pallas_call | solution.py:455
  23.2 4.3 %all-to-all-done.x_ref = bf16[32,32,128]{2,1,0:T(8,128)(2,1)S(1)} async-done(((bf16[32,32,128]{2,1,0:T(8,128)(2,1)}), bf16[32,32,128]{2,1,0:T(8,128)(2,1)S(1)}, u32[]{:S(2)}, u32[]{:S(2)}) %all-to-all-start) | async-done | bytes 262176 | tf_op jit(solution)/shard_map/all_to_all | solution.py:559
  27.6 0.0 copy-start
  27.6 0.0 copy-start.1
  27.6 0.0 copy-start.2
  27.6 7.9 %forward.1 = (bf16[32,64,128]{2,1,0:T(8,128)(2,1)S(1)}, f32[16,128,256]{2,1,0:T(8,128)S(1)}, f32[128,1024]{1,0:T(8,128)S(1)}, bf16[128,1024]{1,0:T(8,128)(2,1)S(1)}) custom-call(s32[2]{0:T(128)S(1)} %pad_add_fusion.where_ref, bf16[32,32,128]{2,1,0:T(8,128)(2,1)S(1)} %all-to-all-done.x_ref, f32[16,128,256]{2,1,0:T(8,128)} %get-tuple-element.24.filter_from, ...), custom_call_target="tpu_custom_call" | custom-call | flops 8589934592 | bytes 1048576 | tf_op jit(solution)/shard_map/forward/pallas_call | solution.py:455
  35.5 15.1 %all_to_all.15.got_ref = bf16[32,64,128]{2,1,0:T(8,128)(2,1)S(1)} all-to-all(bf16[32,64,128]{2,1,0:T(8,128)(2,1)S(1)} %get-tuple-element.27), channel_id=1, replica_groups=mesh['ctx'=32,'ch'=4] {'ctx'}, dimensions={0} | all-to-all | bytes 1048576 | tf_op jit(solution)/shard_map/all_to_all | solution.py:559
  50.6 9.1 %middle.1 = (f32[128,1024]{1,0:T(8,128)}, bf16[128,1024]{1,0:T(8,128)(2,1)}, bf16[128,1024]{1,0:T(8,128)(2,1)}, bf16[128,1024]{1,0:T(8,128)(2,1)}, bf16[32,80,12...) custom-call(s32[2]{0:T(128)S(1)} %pad_add_fusion.where_ref, bf16[32,64,128]{2,1,0:T(8,128)(2,1)S(1)} %all_to_all.15.got_ref, ...), custom_call_target="tpu_custom_call" | custom-call | flops 8589934592 | bytes 1048576 | tf_op jit(solution)/shard_map/middle/pallas_call | solution.py:455
  59.7 0.1 collective-permute-start.3
  59.8 0.9 %collective-permute-start.4 = (bf16[128,1024]{1,0:T(8,128)(2,1)}, bf16[128,1024]{1,0:T(8,128)(2,1)S(1)}, u32[]{:S(2)}, u32[]{:S(2)}) collective-permute-start(bf16[128,1024]{1,0:T(8,128)(2,1)} %get-tuple-element.33), channel_id=1, source_target_pairs={{0,2},{1,3},{2,0},{3,1},{4,6},{5,7},{6,4},{7,5},{8,10},{9,11},{10,... | collective-permute-start | bytes 786440 | tf_op jit(solution)/shard_map/ppermute | solution.py:555
  60.7 1.8 %collective-permute-start.5 = (bf16[128,1024]{1,0:T(8,128)(2,1)}, bf16[128,1024]{1,0:T(8,128)(2,1)S(1)}, u32[]{:S(2)}, u32[]{:S(2)}) collective-permute-start(bf16[128,1024]{1,0:T(8,128)(2,1)} %get-tuple-element.34), channel_id=1, source_target_pairs={{0,3},{1,0},{2,1},{3,2},{4,7},{5,4},{6,5},{7,6},{8,11},{9,8},{10,9... | collective-permute-start | bytes 786440 | tf_op jit(solution)/shard_map/ppermute | solution.py:555
  62.5 4.6 %all-to-all-start.2 = ((bf16[32,80,128]{2,1,0:T(8,128)(2,1)}), bf16[32,80,128]{2,1,0:T(8,128)(2,1)S(1)}, u32[]{:S(2)}, u32[]{:S(2)}) async-start(bf16[32,80,128]{2,1,0:T(8,128)(2,1)} %get-tuple-element.36), calls=%async_computation.2 | async-start | bytes 1310720 | tf_op jit(solution)/shard_map/all_to_all | solution.py:559
  67.0 7.2 %collective-permute-done.3.one_ref = bf16[128,1024]{1,0:T(8,128)(2,1)S(1)} collective-permute-done((bf16[128,1024]{1,0:T(8,128)(2,1)}, bf16[128,1024]{1,0:T(8,128)(2,1)S(1)}, u32[]{:S(2)}, u32[]{:S(2)}) %collective-permute-start.3) | collective-permute-done | bytes 262176 | tf_op jit(solution)/shard_map/ppermute | solution.py:555
  74.3 0.3 collective-permute-done.5.three_ref
  74.6 1.9 %mixed.1 = bf16[128,1024]{1,0:T(8,128)(2,1)} custom-call(f32[128,1024]{1,0:T(8,128)} %get-tuple-element.31.own_from, bf16[128,1024]{1,0:T(8,128)(2,1)S(1)} %collective-permute-done.3.one_ref, bf16[128,1024]{1,0:T(8,128)(2,1)S(1)} %collective-permute-done.4.two_ref, bf16[128,1024]{1,0:T(8,128)(2,1)S(1)} %collective-permute-done.5.three_ref), custom_call_target="tpu_custom_call" | custom-call | flops 68719476736 | bytes 1048576 | tf_op jit(solution)/shard_map/mixed/pallas_call | solution.py:455
  76.5 3.6 %all-to-all-done.2.got_ref = bf16[32,80,128]{2,1,0:T(8,128)(2,1)S(1)} async-done(((bf16[32,80,128]{2,1,0:T(8,128)(2,1)}), bf16[32,80,128]{2,1,0:T(8,128)(2,1)S(1)}, u32[]{:S(2)}, u32[]{:S(2)}) %all-to-all-start.2) | async-done | bytes 655392 | tf_op jit(solution)/shard_map/all_to_all | solution.py:559
  80.1 1.2 %finish.1 = (bf16[128,1024]{1,0:T(8,128)(2,1)}, bf16[128,1024]{1,0:T(8,128)(2,1)}, f32[128,1024]{1,0:T(8,128)}, f32[8,128]{1,0:T(8,128)}) custom-call(bf16[32,80,128]{2,1,0:T(8,128)(2,1)S(1)} %all-to-all-done.2.got_ref, bf16[128,1024]{1,0:T(8,128)(2,1)S(1)} %copy-done, bf16[128,1024]{1,0:T(8,128)(2,1)S(1)} %copy-done.1, ...), custom_call_target="tpu_custom_call" | custom-call | flops 1048576 | bytes 1048576 | tf_op jit(solution)/shard_map/finish/pallas_call | solution.py:455
  (8 shorter events, 0.0 us)
Async XLA Ops:
  0.6 26.9 %collective-permute-start.1 = (bf16[128,1024]{1,0:T(8,128)(2,1)}, bf16[128,1024]{1,0:T(8,128)(2,1)S(1)}, u32[]{:S(2)}, u32[]{:S(2)}) collective-permute-start(bf16[128,1024]{1,0:T(8,128)(2,1)} %cot0_ref.1), channel_id=1, source_target_pairs={{0,2},{1,3},{2,0},{3,1},{4,6},{5,7},{6,4},{7,5},{8,10},{9,11},{10,... | collective-permute-start | bytes 786440 | tf_op jit(solution)/shard_map/ppermute | solution.py:555
  4.3 23.3 %collective-permute-start = (bf16[128,1024]{1,0:T(8,128)(2,1)}, bf16[128,1024]{1,0:T(8,128)(2,1)S(1)}, u32[]{:S(2)}, u32[]{:S(2)}) collective-permute-start(bf16[128,1024]{1,0:T(8,128)(2,1)} %cot0_ref.1), channel_id=1, source_target_pairs={{0,1},{1,2},{2,3},{3,0},{4,5},{5,6},{6,7},{7,4},{8,9},{9,10},{10,1... | collective-permute-start | bytes 786440 | tf_op jit(solution)/shard_map/ppermute | solution.py:555
  4.6 22.9 %collective-permute-start.2 = (bf16[128,1024]{1,0:T(8,128)(2,1)}, bf16[128,1024]{1,0:T(8,128)(2,1)S(1)}, u32[]{:S(2)}, u32[]{:S(2)}) collective-permute-start(bf16[128,1024]{1,0:T(8,128)(2,1)} %cot0_ref.1), channel_id=1, source_target_pairs={{0,3},{1,0},{2,1},{3,2},{4,7},{5,4},{6,5},{7,6},{8,11},{9,8},{10,9... | collective-permute-start | bytes 786440 | tf_op jit(solution)/shard_map/ppermute | solution.py:555
  8.9 18.7 %copy-start.3 = (bf16[128,1024]{1,0:T(8,128)(2,1)S(1)}, bf16[128,1024]{1,0:T(8,128)(2,1)}, u32[]{:S(2)}) copy-start(bf16[128,1024]{1,0:T(8,128)(2,1)} %query_ref.3) | copy-start | bytes 786436
  8.9 18.7 %all-to-all-start = ((bf16[32,32,128]{2,1,0:T(8,128)(2,1)}), bf16[32,32,128]{2,1,0:T(8,128)(2,1)S(1)}, u32[]{:S(2)}, u32[]{:S(2)}) async-start(bf16[32,32,128]{2,1,0:T(8,128)(2,1)} %product.1), calls=%async_computation | async-start | bytes 524288 | tf_op jit(solution)/shard_map/all_to_all | solution.py:559
  27.6 23.0 %copy-start = (bf16[128,1024]{1,0:T(8,128)(2,1)S(1)}, bf16[128,1024]{1,0:T(8,128)(2,1)}, u32[]{:S(2)}) copy-start(bf16[128,1024]{1,0:T(8,128)(2,1)} %key_ref.5) | copy-start | bytes 786436
  27.6 23.0 %copy-start.1 = (bf16[128,1024]{1,0:T(8,128)(2,1)S(1)}, bf16[128,1024]{1,0:T(8,128)(2,1)}, u32[]{:S(2)}) copy-start(bf16[128,1024]{1,0:T(8,128)(2,1)} %value_ref.5) | copy-start | bytes 786436
  27.6 23.0 %copy-start.2 = (f32[1024]{0:T(1024)S(1)}, f32[1024]{0:T(1024)}, u32[]{:S(2)}) copy-start(f32[1024]{0:T(1024)} %param.17) | copy-start | bytes 12292
  59.7 14.5 %collective-permute-start.3 = (bf16[128,1024]{1,0:T(8,128)(2,1)}, bf16[128,1024]{1,0:T(8,128)(2,1)S(1)}, u32[]{:S(2)}, u32[]{:S(2)}) collective-permute-start(bf16[128,1024]{1,0:T(8,128)(2,1)} %get-tuple-element.32), channel_id=1, source_target_pairs={{0,1},{1,2},{2,3},{3,0},{4,5},{5,6},{6,7},{7,4},{8,9},{9,10},{10,1... | collective-permute-start | bytes 786440 | tf_op jit(solution)/shard_map/ppermute | solution.py:555
  59.8 14.5 %collective-permute-start.4 = (bf16[128,1024]{1,0:T(8,128)(2,1)}, bf16[128,1024]{1,0:T(8,128)(2,1)S(1)}, u32[]{:S(2)}, u32[]{:S(2)}) collective-permute-start(bf16[128,1024]{1,0:T(8,128)(2,1)} %get-tuple-element.33), channel_id=1, source_target_pairs={{0,2},{1,3},{2,0},{3,1},{4,6},{5,7},{6,4},{7,5},{8,10},{9,11},{10,... | collective-permute-start | bytes 786440 | tf_op jit(solution)/shard_map/ppermute | solution.py:555
  60.7 13.9 %collective-permute-start.5 = (bf16[128,1024]{1,0:T(8,128)(2,1)}, bf16[128,1024]{1,0:T(8,128)(2,1)S(1)}, u32[]{:S(2)}, u32[]{:S(2)}) collective-permute-start(bf16[128,1024]{1,0:T(8,128)(2,1)} %get-tuple-element.34), channel_id=1, source_target_pairs={{0,3},{1,0},{2,1},{3,2},{4,7},{5,4},{6,5},{7,6},{8,11},{9,8},{10,9... | collective-permute-start | bytes 786440 | tf_op jit(solution)/shard_map/ppermute | solution.py:555
  62.5 17.6 %all-to-all-start.2 = ((bf16[32,80,128]{2,1,0:T(8,128)(2,1)}), bf16[32,80,128]{2,1,0:T(8,128)(2,1)S(1)}, u32[]{:S(2)}, u32[]{:S(2)}) async-start(bf16[32,80,128]{2,1,0:T(8,128)(2,1)} %get-tuple-element.36), calls=%async_computation.2 | async-start | bytes 1310720 | tf_op jit(solution)/shard_map/all_to_all | solution.py:559

commit v2 on v1

v2 whole, which is shorter than its diff:
```python
from functools import partial

import jax
import jax.numpy as jnp
import ml_dtypes
import numpy as np
from jax import lax
from jax.experimental import pallas as pl
from jax.experimental.pallas import tpu as pltpu
from jax.sharding import PartitionSpec as P

PANEL = 128
PANELS = 32
TURNS = 2 * PANELS
OWN = 32
PITCH = 40
CHB = 1024
SPLIT = 4
CHUNK = 256
GROUP = 8
TAIL = 16
F32 = jnp.float32
BF16 = jnp.bfloat16
LIMIT = 24 * 1024 * 1024


def tables():
    freq = np.arange(PANEL) + 0.5
    angle = 2 * np.pi * np.arange(PANEL)[:, None] * freq[None, :] / (2 * PANEL)
    turn = 2 * np.pi * np.arange(TURNS)[:, None] * np.arange(PANELS)[None, :] / TURNS
    cos, sin = np.cos(angle), np.sin(angle)
    inner = np.block([[cos, -sin], [sin, cos]])
    inner_back = np.concatenate([cos.T, -sin.T], axis=0) / (PANEL * TURNS)
    cos, sin = np.cos(turn), np.sin(turn)
    outer = np.concatenate([cos, -sin], axis=0)
    outer_back = np.block([[cos.T, -sin.T], [sin.T, cos.T]])
    return [m.astype(ml_dtypes.bfloat16) for m in (outer, inner, outer_back, inner_back)]


def dot(left, right):
    return jnp.dot(left, right, preferred_element_type=F32)


def dot_rows(left, right):
    return lax.dot_general(left, right, (((1,), (1,)), ((), ())), preferred_element_type=F32)


def spectrum(mid_ref, outer, inner, store):
    for c in range(0, OWN, 4):
        rows = []
        for b in (c, c + 2):
            pair = [mid_ref[0, pl.ds(b + q, PANELS, stride=PITCH), :].astype(BF16) for q in (0, 1)]
            both = dot(outer, jnp.concatenate(pair, axis=1)).astype(BF16)
            for q in (0, 1):
                one = both[:, q * PANEL : (q + 1) * PANEL]
                rows.append(jnp.concatenate([one[:TURNS], one[TURNS:]], axis=1))
        store(c, dot(jnp.concatenate(rows, axis=0), inner).astype(BF16))


def rows_of(freq_ref, c):
    both = freq_ref[pl.ds(c * TURNS, TURNS), :].astype(F32)
    return both[:, :PANEL], both[:, PANEL:]


def spread(c, columns, outer_back, mid_ref):
    back = dot(outer_back, jnp.concatenate(columns, axis=1))
    for part in (0, 1):
        for q in range(len(columns)):
            mid_ref[part, pl.ds(c + q, PANELS, stride=PITCH), :] = back[
                part * PANELS : (part + 1) * PANELS, q * PANEL : (q + 1) * PANEL
            ]


def gather_panels(mid_ref, inner_back, shift, store):
    lanes = lax.broadcasted_iota(jnp.int32, (1, PANEL), 1)
    sign = (1.0 - 2.0 * (lanes % 2).astype(F32)) * shift
    for a in range(0, PANELS, GROUP):
        parts = []
        for b in range(a, a + GROUP):
            real = mid_ref[0, pl.ds(b * PITCH, OWN), :]
            imag = mid_ref[1, pl.ds(b * PITCH, OWN), :]
            other = b - shift
            if 0 <= other < PANELS:
                there_real = mid_ref[0, pl.ds(other * PITCH, OWN), :]
                there_imag = mid_ref[1, pl.ds(other * PITCH, OWN), :]
                real = real - sign * there_imag
                imag = imag + sign * there_real
            parts.append(jnp.concatenate([real.astype(BF16), imag.astype(BF16)], axis=1))
        done = dot(jnp.concatenate(parts, axis=0), inner_back)
        for b in range(GROUP):
            store(a + b, done[b * OWN : (b + 1) * OWN])


def start_all(moves, sems, first=0):
    copies = [pltpu.make_async_copy(here, to, sems.at[first + n]) for n, (here, to) in enumerate(moves)]
    for copy in copies:
        copy.start()
    return copies


def wait_all(copies):
    for copy in copies:
        copy.wait()


def product_kernel(key_from, value_from, out_ref, key_ref, value_ref, sems):
    wait_all(start_all([(key_from, key_ref), (value_from, value_ref)], sems))
    product = key_ref[...].astype(F32) * value_ref[...].astype(F32)
    out_ref[...] = product.T.astype(BF16).reshape(PANELS, OWN, PANEL)


def filter_kernel(
    where_ref,
    raw_from,
    decay_from,
    skip_from,
    outer_from,
    inner_from,
    query_from,
    freq_to,
    rate_ref,
    own_skip_ref,
    outer_ref,
    inner_ref,
    turned_ref,
    freq_ref,
    raw_ref,
    decay_ref,
    skip_ref,
    query_ref,
    mid_ref,
    sems,
):
    column = pl.ds(pl.multiple_of(lax.div(where_ref[0], SPLIT) * PANEL, PANEL), PANEL)
    moves = [(decay_from, decay_ref)]
    for n in range(SPLIT):
        rows = pl.ds(n * CHB, CHB)
        moves.append((raw_from.at[rows, column], raw_ref.at[rows, :]))
    moves += [(outer_from, outer_ref), (inner_from, inner_ref), (skip_from, skip_ref)]
    moves.append((query_from, query_ref))
    loads = start_all(moves, sems)
    place = lax.rem(where_ref[0], SPLIT) * OWN
    row = lax.broadcasted_iota(jnp.int32, (OWN, PANEL), 0)
    lane = lax.broadcasted_iota(jnp.int32, (OWN, PANEL), 1)
    mine = lane == row + place
    choose = mine.astype(BF16)
    loads[0].wait()

    def own_column(ref):
        line = ref[pl.ds(lax.div(where_ref[0], SPLIT), 1), :]
        column = jnp.sum(jnp.where(mine, line, 0.0), axis=1, keepdims=True)
        return jnp.broadcast_to(column, (OWN, PANEL))

    rate = own_column(decay_ref)
    rate_ref[...] = rate
    for n in range(SPLIT):
        loads[1 + n].wait()
        for a in range(n * GROUP, (n + 1) * GROUP, 4):
            chosen = dot_rows(choose, raw_ref[pl.ds(a * PANEL, 4 * PANEL), :])
            for b in range(4):
                spot = (lane + (a + b) * PANEL).astype(F32)
                taps = chosen[:, b * PANEL : (b + 1) * PANEL] * jnp.exp(-rate * spot)
                mid_ref[0, pl.ds((a + b) * PITCH, OWN), :] = taps
    wait_all(loads[1 + SPLIT :])
    own_skip_ref[...] = own_column(skip_ref)
    for c in range(0, CHB, CHUNK):
        at = pl.ds(c, CHUNK)
        turned_ref[at, :] = query_ref[:, at].astype(F32).T.astype(BF16)
    writes = []

    def store(c, rows):
        part = pl.ds(c * TURNS, 4 * TURNS)
        freq_ref[part, :] = rows
        writes.extend(start_all([(freq_ref.at[part], freq_to.at[part])], sems, len(moves) + len(writes)))

    spectrum(mid_ref, outer_ref[...], inner_ref[...], store)
    wait_all(writes)


def forward_kernel(
    where_ref,
    x_ref,
    own_skip_ref,
    outer_ref,
    inner_ref,
    query_ref,
    cot1_ref,
    cot2_ref,
    cot3_ref,
    cot0_ref,
    filter_from,
    outer_back_from,
    inner_back_from,
    weight_from,
    send_ref,
    freq_ref,
    back_ref,
    mid_ref,
    outer_back_ref,
    inner_back_ref,
    filter_ref,
    cot_ref,
    weight_ref,
    sems,
):
    moves = [
        (outer_back_from, outer_back_ref),
        (inner_back_from, inner_back_ref),
        (filter_from, filter_ref),
    ]
    moves += [(ref, cot_ref.at[s]) for s, ref in enumerate((cot0_ref, cot1_ref, cot2_ref, cot3_ref))]
    loads = start_all(moves, sems)

    def weight_copy(n):
        rows = pl.ds(pl.multiple_of(n * CHUNK, CHUNK), CHUNK)
        return pltpu.make_async_copy(
            weight_from.at[rows, :], weight_ref.at[rows, :], sems.at[len(moves) + n]
        )

    for n in range(CHB // CHUNK):
        weight_copy(n).start()
    for a in range(PANELS):
        mid_ref[0, pl.ds(a * PITCH, OWN), :] = x_ref[a].astype(F32)

    def store(c, rows):
        freq_ref[pl.ds(c * TURNS, 4 * TURNS), :] = rows

    spectrum(mid_ref, outer_ref[...], inner_ref[...], store)
    wait_all(loads[:3])
    outer_back = outer_back_ref[...]
    for c in range(0, OWN, 2):
        columns = []
        for b in (c, c + 1):
            xr, xi = rows_of(freq_ref, b)
            hr, hi = rows_of(filter_ref, b)
            columns.append(
                jnp.concatenate(
                    [(hr * xr - hi * xi).astype(BF16), (hr * xi + hi * xr).astype(BF16)], axis=0
                )
            )
        spread(c, columns, outer_back, mid_ref)

    own_skip = own_skip_ref[...]

    def store_panel(a, value):
        send_ref[a, :OWN, :] = (value + own_skip * x_ref[a].astype(F32)).astype(BF16)

    gather_panels(mid_ref, inner_back_ref[...], 1, store_panel)
    wait_all(loads[3:])
    starts = [lax.rem(where_ref[1] + SPLIT - s, SPLIT) * CHB for s in range(SPLIT)]
    columns = [pl.ds(pl.multiple_of(start, CHB), CHB) for start in starts]

    @pl.loop(0, CHB // CHUNK)
    def _(n):
        weight_copy(n).wait()
        at = pl.ds(pl.multiple_of(n * CHUNK, CHUNK), CHUNK)
        total = dot_rows(weight_ref[at, columns[0]], cot_ref[0])
        for s in range(1, SPLIT):
            total += dot_rows(weight_ref[at, columns[s]], cot_ref[s])
        back_ref[at, :] = total
        grad = (query_ref[at, :].astype(F32) * total).astype(BF16)
        for b in range(CHUNK // OWN):
            send_ref[n * (CHUNK // OWN) + b, OWN:, :] = grad[b * OWN : (b + 1) * OWN]


def middle_kernel(
    where_ref,
    got_ref,
    x_ref,
    freq_ref,
    rate_ref,
    own_skip_ref,
    outer_ref,
    inner_ref,
    query_ref,
    back_ref,
    filter_from,
    outer_back_from,
    inner_back_from,
    weight_from,
    own_to,
    one_to,
    two_to,
    three_to,
    send_to,
    d_query_to,
    outer_back_ref,
    inner_back_ref,
    filter_ref,
    spec_ref,
    mid_ref,
    lag_ref,
    gated_ref,
    d_query_ref,
    part_ref,
    send_ref,
    weight_ref,
    sems,
):
    moves = [
        (outer_back_from, outer_back_ref),
        (inner_back_from, inner_back_ref),
        (filter_from, filter_ref),
    ]
    loads = start_all(moves, sems)
    writes = []

    def write(this, to):
        writes.extend(start_all([(this, to)], sems, len(moves) + SPLIT + len(writes)))

    def weight_copy(n, s):
        block = lax.rem(where_ref[1] + s, SPLIT) * CHB
        columns = pl.ds(pl.multiple_of(block, CHB), CHB)
        return pltpu.make_async_copy(
            weight_from.at[:, columns], weight_ref.at[n], sems.at[len(moves) + n]
        )

    for n, s in enumerate((2, 1, 3, 0)):
        weight_copy(n, s).start()
    for c in range(0, CHB, CHUNK):
        at = pl.ds(c, CHUNK)
        block = got_ref[pl.ds(c // OWN, CHUNK // OWN), :OWN, :].reshape(CHUNK, PANEL)
        convolved = block.astype(F32)
        gated_ref[:, at] = (query_ref[at, :].astype(F32) * convolved).T.astype(BF16)
        d_query_ref[:, at] = (back_ref[at, :] * convolved).T.astype(BF16)
    write(d_query_ref, d_query_to)
    for a in range(PANELS):
        mid_ref[0, pl.ds(a * PITCH, OWN), :] = got_ref[a, OWN:, :].astype(F32)

    def store(c, rows):
        spec_ref[pl.ds(c * TURNS, 4 * TURNS), :] = rows

    spectrum(mid_ref, outer_ref[...], inner_ref[...], store)
    wait_all(loads)
    outer_back = outer_back_ref[...]
    for c in range(0, OWN, 2):
        columns = {0: [], 1: []}
        for b in (c, c + 1):
            gr, gi = rows_of(spec_ref, b)
            for n, other_ref in enumerate((filter_ref, freq_ref)):
                hr, hi = rows_of(other_ref, b)
                columns[n].append(
                    jnp.concatenate(
                        [(gr * hr + gi * hi).astype(BF16), (gi * hr - gr * hi).astype(BF16)], axis=0
                    )
                )
        spread(c, columns[0], outer_back, mid_ref)
        spread(c, columns[1], outer_back, lag_ref)
    own_skip = own_skip_ref[...]
    sums = [jnp.zeros((OWN, PANEL), F32)]

    def store_input(a, value):
        grad = got_ref[a, OWN:, :].astype(F32)
        sums[0] += grad * x_ref[a].astype(F32)
        send_ref[a, :OWN, :] = (value + own_skip * grad).astype(BF16)

    gather_panels(mid_ref, inner_back_ref[...], -1, store_input)
    rate = rate_ref[...]
    lane = lax.broadcasted_iota(jnp.int32, (OWN, PANEL), 1)
    row = lax.broadcasted_iota(jnp.int32, (OWN, PANEL), 0)
    total = jnp.sum(sums[0], axis=1, keepdims=True)
    place = lax.rem(where_ref[0], SPLIT) * OWN
    line = jnp.sum(jnp.where(lane == row + place, total, 0.0), axis=0, keepdims=True)
    high = line.astype(BF16).astype(F32)
    index = lax.broadcasted_iota(jnp.int32, (TAIL, PANEL), 0)
    tail = jnp.where(index == 0, high, jnp.where(index == 1, line - high, 0.0)).astype(BF16)

    def store_lag(a, value):
        window = jnp.exp(-rate * (lane + a * PANEL).astype(F32))
        send_ref[a, OWN : 2 * OWN, :] = (value * window).astype(BF16)
        send_ref[a, 2 * OWN :, :] = tail
        if (a + 1) % GROUP == 0:
            part = pl.ds(a + 1 - GROUP, GROUP)
            write(send_ref.at[part], send_to.at[part])

    gather_panels(lag_ref, inner_back_ref[...], -1, store_lag)
    outs = (two_to, one_to, three_to, own_to)
    base = len(moves) + SPLIT + len(writes)
    writes += [
        pltpu.make_async_copy(part_ref.at[n], to, sems.at[base + n]) for n, to in enumerate(outs)
    ]

    @pl.loop(0, SPLIT)
    def _(n):
        weight_copy(n, 0).wait()
        for c in range(0, CHB, CHUNK):
            at = pl.ds(c, CHUNK)
            part_ref[n, :, at] = dot(gated_ref[...], weight_ref[n, :, at]).astype(BF16)
        for k in range(SPLIT):

            @pl.when(n == k)
            def _():
                writes[k - SPLIT].start()

    wait_all(writes)


def mixed_kernel(own_from, one_ref, two_ref, three_ref, mixed_ref, own_ref, sem):
    copy = pltpu.make_async_copy(own_from, own_ref, sem)
    copy.start()
    copy.wait()
    for c in range(0, CHB, CHUNK):
        at = pl.ds(c, CHUNK)
        mixed = own_ref[:, at].astype(F32) + one_ref[:, at].astype(F32)
        mixed += two_ref[:, at].astype(F32) + three_ref[:, at].astype(F32)
        mixed_ref[:, at] = mixed.astype(BF16)


def finish_kernel(got_ref, key_ref, value_ref, d_key_ref, d_value_ref, lag_ref, skip_grad_ref):
    for c in range(0, CHB, CHUNK):
        at = pl.ds(c, CHUNK)
        block = pl.ds(c // OWN, CHUNK // OWN)
        lag_ref[:, at] = got_ref[block, OWN : 2 * OWN, :].reshape(CHUNK, PANEL).astype(F32).T
        grad = got_ref[block, :OWN, :].reshape(CHUNK, PANEL).astype(F32).T
        d_key_ref[:, at] = (grad * value_ref[:, at].astype(F32)).astype(BF16)
        d_value_ref[:, at] = (grad * key_ref[:, at].astype(F32)).astype(BF16)
    for r in range(PANELS // SPLIT):
        line = jnp.zeros((1, PANEL), F32)
        for b in range(SPLIT):
            tail = got_ref[r * SPLIT + b, 2 * OWN :, :].astype(F32)
            line += tail[0:1] + tail[1:2]
        skip_grad_ref[pl.ds(r, 1), :] = line


VMEM = pl.BlockSpec(memory_space=pltpu.VMEM)
SMEM = pl.BlockSpec(memory_space=pltpu.SMEM)
HBM = pl.BlockSpec(memory_space=pltpu.HBM)
ANY = pl.BlockSpec(memory_space=pl.ANY)
NEAR = pl.BlockSpec(memory_space=pltpu.VMEM)
FREQ = (OWN * TURNS, 2 * PANEL)
MID = pltpu.VMEM((2, PANELS * PITCH, PANEL), F32)
BLOCK = (PANEL, CHB)
SENT = (PANELS, 2 * OWN, PANEL)
LAST = (PANELS, 2 * OWN + TAIL, PANEL)


def shape(dims, kind):
    return jax.ShapeDtypeStruct(dims, kind)


def here(dims, kind):
    return pltpu.VMEM(dims, kind)


def far(dims, kind):
    return pltpu.HBM(dims, kind)


def call(kernel, in_specs, out_shape, scratch, flops, name, out_specs=None):
    run = pl.pallas_call(
        kernel,
        in_specs=in_specs,
        out_specs=out_specs or jax.tree.map(lambda _: VMEM, out_shape),
        out_shape=out_shape,
        scratch_shapes=scratch,
        compiler_params=pltpu.CompilerParams(vmem_limit_bytes=LIMIT),
        cost_estimate=pl.CostEstimate(flops=flops, bytes_accessed=1 << 20, transcendentals=0),
        name=name,
    )

    def placed(arg, spec):
        if spec is HBM:
            return pltpu.with_memory_space_constraint(arg, pltpu.HBM)
        if spec is NEAR:
            return pltpu.with_memory_space_constraint(arg, pltpu.VMEM)
        return arg

    def bound(*args):
        return run(*(placed(arg, spec) for arg, spec in zip(args, in_specs, strict=True)))

    return bound


def sems(count):
    return pltpu.SemaphoreType.DMA((count,))


def make_product(key_in, value_in):
    scratch = [pltpu.VMEM(BLOCK, BF16), pltpu.VMEM(BLOCK, BF16), sems(2)]
    out = shape((PANELS, OWN, PANEL), BF16)
    return call(product_kernel, [HBM] * 2, out, scratch, 1 << 20, "product")(key_in, value_in)


def make_filter(where, filter_raw, decay, skip, outer, inner, query):
    out = [far(FREQ, BF16), here((OWN, PANEL), F32), here((OWN, PANEL), F32)]
    out += [here(m.shape, BF16) for m in (outer, inner)] + [here((CHB, PANEL), BF16)]
    scratch = [
        pltpu.VMEM(FREQ, BF16),
        pltpu.VMEM((PANELS * PANEL, PANEL), BF16),
        pltpu.VMEM(decay.shape, F32),
        pltpu.VMEM(skip.shape, F32),
        pltpu.VMEM(BLOCK, BF16),
        MID,
        sems(5 + SPLIT + OWN // 4),
    ]
    specs = [SMEM] + [HBM] * 6
    return call(filter_kernel, specs, out, scratch, 1 << 32, "taps", [HBM] + [VMEM] * 5)(
        where, filter_raw, decay, skip, outer, inner, query
    )


def make_forward(where, x, own_skip, held, query, weight, cots, freq_filter, back_mats):
    out = [shape(SENT, BF16), here(FREQ, BF16), here((CHB, PANEL), F32)]
    scratch = [MID] + [pltpu.VMEM(m.shape, BF16) for m in back_mats]
    scratch += [pltpu.VMEM(FREQ, BF16), pltpu.VMEM((SPLIT, *BLOCK), BF16)]
    scratch += [pltpu.VMEM(weight.shape, BF16), sems(3 + SPLIT + CHB // CHUNK)]
    specs = [SMEM] + [VMEM] * 5 + [ANY] * 3 + [HBM] * 5
    return call(forward_kernel, specs, out, scratch, 1 << 33, "forward")(
        where, x, own_skip, *held, query, *cots[1:], cots[0], freq_filter, *back_mats, weight
    )


def make_middle(where, got, x, freq_x, rate, own_skip, held, query, back, *rest):
    out = [far(BLOCK, BF16)] * 4 + [far(LAST, BF16), far(BLOCK, BF16)]
    scratch = [pltpu.VMEM(m.shape, BF16) for m in rest[1:3]]
    scratch += [pltpu.VMEM(FREQ, BF16), pltpu.VMEM(FREQ, BF16), MID, MID]
    scratch += [pltpu.VMEM(BLOCK, BF16)] * 2
    scratch += [pltpu.VMEM((SPLIT, *BLOCK), BF16), pltpu.VMEM(LAST, BF16)]
    scratch += [pltpu.VMEM((SPLIT, CHB, CHB), BF16), sems(4 + 2 * SPLIT + PANELS // GROUP)]
    specs = [SMEM] + [VMEM] * 9 + [HBM] * 4
    return call(middle_kernel, specs, out, scratch, 1 << 33, "middle", [HBM] * 6)(
        where, got, x, freq_x, rate, own_skip, *held, query, back, *rest
    )


def make_mixed(parts):
    scratch = [pltpu.VMEM(BLOCK, BF16), pltpu.SemaphoreType.DMA]
    specs = [HBM] + [VMEM] * 3
    return call(mixed_kernel, specs, shape(BLOCK, BF16), scratch, 1 << 36, "mixed")(*parts)


def make_finish(got, key_in, value_in):
    out = [shape(BLOCK, BF16)] * 2 + [shape(BLOCK, F32), shape((CHB // PANEL, PANEL), F32)]
    return call(finish_kernel, [VMEM] * 3, out, [], 1 << 20, "finish")(got, key_in, value_in)


def shifted(value, step):
    return lax.ppermute(value, "ch", [(i, (i + step) % SPLIT) for i in range(SPLIT)])


def exchange(value):
    return lax.all_to_all(value, "ctx", 0, 0)


def local(query, key_in, value_in, filter_raw, decay, skip, out_weight, cotangent):
    mats = [jnp.asarray(m) for m in tables()]
    where = jnp.stack([lax.axis_index("ctx"), lax.axis_index("ch")]).astype(jnp.int32)
    lines = (CHB // PANEL, PANEL)
    cots = [cotangent] + [shifted(cotangent, s) for s in (1, 2, 3)]
    x = exchange(make_product(key_in, value_in))
    freq_filter, rate, own_skip, *held, turned = make_filter(
        where, filter_raw, decay.reshape(lines), skip.reshape(lines), *mats[:2], query
    )
    send, freq_x, back = make_forward(
        where, x, own_skip, held, turned, out_weight, cots, freq_filter, mats[2:]
    )
    got = exchange(send)
    own, one, two, three, last, d_query = make_middle(
        where, got, x, freq_x, rate, own_skip, held, turned, back, freq_filter, *mats[2:], out_weight
    )
    last = exchange(last)
    mixed = make_mixed([own, shifted(one, 1), shifted(two, 2), shifted(three, 3)])
    d_key, d_value, filter_grad, skip_grad = make_finish(last, key_in, value_in)
    return (mixed, d_query, d_key, d_value, filter_grad, skip_grad.reshape(CHB))


def solution(mesh):
    in_specs = (
        P("ctx", "ch"),
        P("ctx", "ch"),
        P("ctx", "ch"),
        P(None, "ch"),
        P("ch"),
        P("ch"),
        P("ch", None),
        P("ctx", "ch"),
    )
    out_specs = (
        P("ctx", "ch"),
        P("ctx", "ch"),
        P("ctx", "ch"),
        P("ctx", "ch"),
        P("ctx", "ch"),
        P("ch"),
    )
    return jax.shard_map(local, mesh=mesh, in_specs=in_specs, out_specs=out_specs, check_vma=False)
```

time: 81.7 us -> 77 us (0.942)
  Pallas kernels: 26.4 us -> 21.4 us
    pallas_call x6, Pallas kernels: 26.4 us -> 21.4 us  [bound(): run(*(placed(arg, spec) for arg, spec in zip(args, in_specs, strict=True)))]
where the time goes in v2:
time: 77 us; the launch traced here: 76.6 us
  starting transfers between devices  23.3 us (30%)
  Pallas kernels  21.4 us (28%)
  waiting for transfers between devices  16 us (21%)
  blocking collectives  15.1 us (20%)
    pallas_call x6, Pallas kernels, bound(): run(*(placed(arg, spec) for arg, spec in zip(args, in_specs, strict=True)))  21.4 us
    all_to_all x1, blocking collectives, exchange(): return lax.all_to_all(value, 'ctx', 0, 0)  15.1 us
    all_to_all x2, starting transfers between devices, exchange(): return lax.all_to_all(value, 'ctx', 0, 0)  14.2 us
    ppermute x6, starting transfers between devices, shifted(): lax.ppermute(value, 'ch', [(i, (i + step) % SPLIT) for i in range(SPLIT)])  9.07 us
    all_to_all x2, waiting for transfers between devices, exchange(): return lax.all_to_all(value, 'ctx', 0, 0)  8.43 us
    ppermute x6, waiting for transfers between devices, shifted(): lax.ppermute(value, 'ch', [(i, (i + step) % SPLIT) for i in range(SPLIT)])  7.58 us
  transfers between devices with their start and end apart: 8, of which 4 were waited for; matrix products, arithmetic and copies ran while one was open for 0% of the time, Pallas kernels for 10%

profile of v2, /device:TPU:1, one launch (start us, length us, event | category | flops | bytes accessed | tf_op | source)
XLA Modules:
  0.0 76.6 jit_solution(17618176357442203018)
XLA Ops:
  0.6 3.7 %collective-permute-start.1 = (bf16[128,1024]{1,0:T(8,128)(2,1)}, bf16[128,1024]{1,0:T(8,128)(2,1)S(1)}, u32[]{:S(2)}, u32[]{:S(2)}) collective-permute-start(bf16[128,1024]{1,0:T(8,128)(2,1)} %cot0_ref.1), channel_id=1, source_target_pairs={{0,2},{1,3},{2,0},{3,1},{4,6},{5,7},{6,4},{7,5},{8,10},{9,11},{10,... | collective-permute-start | bytes 786440 | tf_op jit(solution)/shard_map/ppermute | solution.py:538
  4.3 0.3 collective-permute-start
  4.6 2.4 %collective-permute-start.2 = (bf16[128,1024]{1,0:T(8,128)(2,1)}, bf16[128,1024]{1,0:T(8,128)(2,1)S(1)}, u32[]{:S(2)}, u32[]{:S(2)}) collective-permute-start(bf16[128,1024]{1,0:T(8,128)(2,1)} %cot0_ref.1), channel_id=1, source_target_pairs={{0,3},{1,0},{2,1},{3,2},{4,7},{5,4},{6,5},{7,6},{8,11},{9,8},{10,9... | collective-permute-start | bytes 786440 | tf_op jit(solution)/shard_map/ppermute | solution.py:538
  7.0 1.9 %product.1 = bf16[32,32,128]{2,1,0:T(8,128)(2,1)} custom-call(bf16[128,1024]{1,0:T(8,128)(2,1)} %key_ref.1, bf16[128,1024]{1,0:T(8,128)(2,1)} %value_ref.1), custom_call_target="tpu_custom_call" | custom-call | flops 1048576 | bytes 1048576 | tf_op jit(solution)/shard_map/product/pallas_call | solution.py:469
  8.9 9.6 %all-to-all-start = ((bf16[32,32,128]{2,1,0:T(8,128)(2,1)}), bf16[32,32,128]{2,1,0:T(8,128)(2,1)S(1)}, u32[]{:S(2)}, u32[]{:S(2)}) async-start(bf16[32,32,128]{2,1,0:T(8,128)(2,1)} %product.1), calls=%async_computation | async-start | bytes 524288 | tf_op jit(solution)/shard_map/all_to_all | solution.py:542
  18.5 0.1 pad_add_fusion.where_ref
  18.6 4.0 %taps.1 = (bf16[2048,256]{1,0:T(8,128)(2,1)}, f32[32,128]{1,0:T(8,128)S(1)}, f32[32,128]{1,0:T(8,128)S(1)}, bf16[128,32]{1,0:T(8,128)(2,1)S(1)}, bf16[256,256]{1...) custom-call(s32[2]{0:T(128)S(1)} %pad_add_fusion.where_ref, bf16[4096,1024]{1,0:T(8,128)(2,1)} %raw_from.1, ...), custom_call_target="tpu_custom_call" | custom-call | flops 4294967296 | bytes 1048576 | tf_op jit(solution)/shard_map/taps/pallas_call | solution.py:469
  22.5 4.8 %all-to-all-done.x_ref = bf16[32,32,128]{2,1,0:T(8,128)(2,1)S(1)} async-done(((bf16[32,32,128]{2,1,0:T(8,128)(2,1)}), bf16[32,32,128]{2,1,0:T(8,128)(2,1)S(1)}, u32[]{:S(2)}, u32[]{:S(2)}) %all-to-all-start) | async-done | bytes 262176 | tf_op jit(solution)/shard_map/all_to_all | solution.py:542
  27.4 0.0 collective-permute-done.1.cot2_ref
  27.4 0.0 collective-permute-done.cot1_ref
  27.4 0.0 collective-permute-done.2.cot3_ref
  27.4 5.7 %forward.1 = (bf16[32,64,128]{2,1,0:T(8,128)(2,1)S(1)}, bf16[2048,256]{1,0:T(8,128)(2,1)S(1)}, f32[1024,128]{1,0:T(8,128)S(1)}) custom-call(s32[2]{0:T(128)S(1)} %pad_add_fusion.where_ref, bf16[32,32,128]{2,1,0:T(8,128)(2,1)S(1)} %all-to-all-done.x_ref, f32[32,128]{1,0:T(8,128)S(1)} %get-tuple-element.25.own_skip_ref, ...), custom_call_target="tpu_custom_call" | custom-call | flops 8589934592 | bytes 1048576 | tf_op jit(solution)/shard_map/forward/pallas_call | solution.py:469
  33.1 15.1 %all_to_all.15.got_ref = bf16[32,64,128]{2,1,0:T(8,128)(2,1)S(1)} all-to-all(bf16[32,64,128]{2,1,0:T(8,128)(2,1)S(1)} %get-tuple-element.30), channel_id=1, replica_groups=mesh['ctx'=32,'ch'=4] {'ctx'}, dimensions={0} | all-to-all | bytes 1048576 | tf_op jit(solution)/shard_map/all_to_all | solution.py:542
  48.3 6.8 %middle.1 = (bf16[128,1024]{1,0:T(8,128)(2,1)}, bf16[128,1024]{1,0:T(8,128)(2,1)}, bf16[128,1024]{1,0:T(8,128)(2,1)}, bf16[128,1024]{1,0:T(8,128)(2,1)}, bf16[32...) custom-call(s32[2]{0:T(128)S(1)} %pad_add_fusion.where_ref, bf16[32,64,128]{2,1,0:T(8,128)(2,1)S(1)} %all_to_all.15.got_ref, ...), custom_call_target="tpu_custom_call" | custom-call | flops 8589934592 | bytes 1048576 | tf_op jit(solution)/shard_map/middle/pallas_call | solution.py:469
  55.1 0.1 collective-permute-start.3
  55.2 0.9 %collective-permute-start.4 = (bf16[128,1024]{1,0:T(8,128)(2,1)}, bf16[128,1024]{1,0:T(8,128)(2,1)S(1)}, u32[]{:S(2)}, u32[]{:S(2)}) collective-permute-start(bf16[128,1024]{1,0:T(8,128)(2,1)} %get-tuple-element.36), channel_id=1, source_target_pairs={{0,2},{1,3},{2,0},{3,1},{4,6},{5,7},{6,4},{7,5},{8,10},{9,11},{10,... | collective-permute-start | bytes 786440 | tf_op jit(solution)/shard_map/ppermute | solution.py:538
  56.1 1.8 %collective-permute-start.5 = (bf16[128,1024]{1,0:T(8,128)(2,1)}, bf16[128,1024]{1,0:T(8,128)(2,1)S(1)}, u32[]{:S(2)}, u32[]{:S(2)}) collective-permute-start(bf16[128,1024]{1,0:T(8,128)(2,1)} %get-tuple-element.37), channel_id=1, source_target_pairs={{0,3},{1,0},{2,1},{3,2},{4,7},{5,4},{6,5},{7,6},{8,11},{9,8},{10,9... | collective-permute-start | bytes 786440 | tf_op jit(solution)/shard_map/ppermute | solution.py:538
  57.8 4.6 %all-to-all-start.2 = ((bf16[32,80,128]{2,1,0:T(8,128)(2,1)}), bf16[32,80,128]{2,1,0:T(8,128)(2,1)S(1)}, u32[]{:S(2)}, u32[]{:S(2)}) async-start(bf16[32,80,128]{2,1,0:T(8,128)(2,1)} %get-tuple-element.39), calls=%async_computation.2 | async-start | bytes 1310720 | tf_op jit(solution)/shard_map/all_to_all | solution.py:542
  62.4 7.2 %collective-permute-done.3.one_ref = bf16[128,1024]{1,0:T(8,128)(2,1)S(1)} collective-permute-done((bf16[128,1024]{1,0:T(8,128)(2,1)}, bf16[128,1024]{1,0:T(8,128)(2,1)S(1)}, u32[]{:S(2)}, u32[]{:S(2)}) %collective-permute-start.3) | collective-permute-done | bytes 262176 | tf_op jit(solution)/shard_map/ppermute | solution.py:538
  69.6 0.0 collective-permute-done.4.two_ref
  69.6 0.3 collective-permute-done.5.three_ref
  70.0 1.9 %mixed.1 = bf16[128,1024]{1,0:T(8,128)(2,1)} custom-call(bf16[128,1024]{1,0:T(8,128)(2,1)} %get-tuple-element.34.own_from, bf16[128,1024]{1,0:T(8,128)(2,1)S(1)} %collective-permute-done.3.one_ref, bf16[128,1024]{1,0:T(8,128)(2,1)S(1)} %collective-permute-done.4.two_ref, bf16[128,1024]{1,0:T(8,128)(2,1)S(1)} %collective-permute-done.5.three_ref), custom_call_target="tpu_custom_call" | custom-call | flops 68719476736 | bytes 1048576 | tf_op jit(solution)/shard_map/mixed/pallas_call | solution.py:469
  71.8 3.6 %all-to-all-done.2.got_ref = bf16[32,80,128]{2,1,0:T(8,128)(2,1)S(1)} async-done(((bf16[32,80,128]{2,1,0:T(8,128)(2,1)}), bf16[32,80,128]{2,1,0:T(8,128)(2,1)S(1)}, u32[]{:S(2)}, u32[]{:S(2)}) %all-to-all-start.2) | async-done | bytes 655392 | tf_op jit(solution)/shard_map/all_to_all | solution.py:542
  75.4 1.2 %finish.1 = (bf16[128,1024]{1,0:T(8,128)(2,1)}, bf16[128,1024]{1,0:T(8,128)(2,1)}, f32[128,1024]{1,0:T(8,128)}, f32[8,128]{1,0:T(8,128)}) custom-call(bf16[32,80,128]{2,1,0:T(8,128)(2,1)S(1)} %all-to-all-done.2.got_ref, bf16[128,1024]{1,0:T(8,128)(2,1)S(1)} %copy-done, bf16[128,1024]{1,0:T(8,128)(2,1)S(1)} %copy-done.1), custom_call_target="tpu_custom_call" | custom-call | flops 1048576 | bytes 1048576 | tf_op jit(solution)/shard_map/finish/pallas_call | solution.py:469
  (4 shorter events, 0.0 us)
Async XLA Ops:
  0.6 26.8 %collective-permute-start.1 = (bf16[128,1024]{1,0:T(8,128)(2,1)}, bf16[128,1024]{1,0:T(8,128)(2,1)S(1)}, u32[]{:S(2)}, u32[]{:S(2)}) collective-permute-start(bf16[128,1024]{1,0:T(8,128)(2,1)} %cot0_ref.1), channel_id=1, source_target_pairs={{0,2},{1,3},{2,0},{3,1},{4,6},{5,7},{6,4},{7,5},{8,10},{9,11},{10,... | collective-permute-start | bytes 786440 | tf_op jit(solution)/shard_map/ppermute | solution.py:538
  4.3 23.1 %collective-permute-start = (bf16[128,1024]{1,0:T(8,128)(2,1)}, bf16[128,1024]{1,0:T(8,128)(2,1)S(1)}, u32[]{:S(2)}, u32[]{:S(2)}) collective-permute-start(bf16[128,1024]{1,0:T(8,128)(2,1)} %cot0_ref.1), channel_id=1, source_target_pairs={{0,1},{1,2},{2,3},{3,0},{4,5},{5,6},{6,7},{7,4},{8,9},{9,10},{10,1... | collective-permute-start | bytes 786440 | tf_op jit(solution)/shard_map/ppermute | solution.py:538
  4.6 22.8 %collective-permute-start.2 = (bf16[128,1024]{1,0:T(8,128)(2,1)}, bf16[128,1024]{1,0:T(8,128)(2,1)S(1)}, u32[]{:S(2)}, u32[]{:S(2)}) collective-permute-start(bf16[128,1024]{1,0:T(8,128)(2,1)} %cot0_ref.1), channel_id=1, source_target_pairs={{0,3},{1,0},{2,1},{3,2},{4,7},{5,4},{6,5},{7,6},{8,11},{9,8},{10,9... | collective-permute-start | bytes 786440 | tf_op jit(solution)/shard_map/ppermute | solution.py:538
  8.9 18.5 %all-to-all-start = ((bf16[32,32,128]{2,1,0:T(8,128)(2,1)}), bf16[32,32,128]{2,1,0:T(8,128)(2,1)S(1)}, u32[]{:S(2)}, u32[]{:S(2)}) async-start(bf16[32,32,128]{2,1,0:T(8,128)(2,1)} %product.1), calls=%async_computation | async-start | bytes 524288 | tf_op jit(solution)/shard_map/all_to_all | solution.py:542
  55.1 14.5 %collective-permute-start.3 = (bf16[128,1024]{1,0:T(8,128)(2,1)}, bf16[128,1024]{1,0:T(8,128)(2,1)S(1)}, u32[]{:S(2)}, u32[]{:S(2)}) collective-permute-start(bf16[128,1024]{1,0:T(8,128)(2,1)} %get-tuple-element.35), channel_id=1, source_target_pairs={{0,1},{1,2},{2,3},{3,0},{4,5},{5,6},{6,7},{7,4},{8,9},{9,10},{10,1... | collective-permute-start | bytes 786440 | tf_op jit(solution)/shard_map/ppermute | solution.py:538
  55.2 14.5 %collective-permute-start.4 = (bf16[128,1024]{1,0:T(8,128)(2,1)}, bf16[128,1024]{1,0:T(8,128)(2,1)S(1)}, u32[]{:S(2)}, u32[]{:S(2)}) collective-permute-start(bf16[128,1024]{1,0:T(8,128)(2,1)} %get-tuple-element.36), channel_id=1, source_target_pairs={{0,2},{1,3},{2,0},{3,1},{4,6},{5,7},{6,4},{7,5},{8,10},{9,11},{10,... | collective-permute-start | bytes 786440 | tf_op jit(solution)/shard_map/ppermute | solution.py:538
  56.1 13.9 %collective-permute-start.5 = (bf16[128,1024]{1,0:T(8,128)(2,1)}, bf16[128,1024]{1,0:T(8,128)(2,1)S(1)}, u32[]{:S(2)}, u32[]{:S(2)}) collective-permute-start(bf16[128,1024]{1,0:T(8,128)(2,1)} %get-tuple-element.37), channel_id=1, source_target_pairs={{0,3},{1,0},{2,1},{3,2},{4,7},{5,4},{6,5},{7,6},{8,11},{9,8},{10,9... | collective-permute-start | bytes 786440 | tf_op jit(solution)/shard_map/ppermute | solution.py:538
  57.8 17.6 %all-to-all-start.2 = ((bf16[32,80,128]{2,1,0:T(8,128)(2,1)}), bf16[32,80,128]{2,1,0:T(8,128)(2,1)S(1)}, u32[]{:S(2)}, u32[]{:S(2)}) async-start(bf16[32,80,128]{2,1,0:T(8,128)(2,1)} %get-tuple-element.39), calls=%async_computation.2 | async-start | bytes 1310720 | tf_op jit(solution)/shard_map/all_to_all | solution.py:542
  70.0 5.5 %copy-start = (bf16[128,1024]{1,0:T(8,128)(2,1)S(1)}, bf16[128,1024]{1,0:T(8,128)(2,1)}, u32[]{:S(2)}) copy-start(bf16[128,1024]{1,0:T(8,128)(2,1)} %key_ref.1) | copy-start | bytes 786436
  70.0 5.5 %copy-start.1 = (bf16[128,1024]{1,0:T(8,128)(2,1)S(1)}, bf16[128,1024]{1,0:T(8,128)(2,1)}, u32[]{:S(2)}) copy-start(bf16[128,1024]{1,0:T(8,128)(2,1)} %value_ref.1) | copy-start | bytes 786436

commit v3 on v2

--- a/solution.py
+++ b/solution.py
@@ -117,17 +117,23 @@
     outer_from,
     inner_from,
     query_from,
+    cot_from,
+    weight_from,
     freq_to,
     rate_ref,
     own_skip_ref,
     outer_ref,
     inner_ref,
     turned_ref,
+    share_to,
     freq_ref,
     raw_ref,
     decay_ref,
     skip_ref,
     query_ref,
+    cot_ref,
+    keep_ref,
+    share_ref,
     mid_ref,
     sems,
 ):
@@ -137,7 +143,8 @@
         rows = pl.ds(n * CHB, CHB)
         moves.append((raw_from.at[rows, column], raw_ref.at[rows, :]))
     moves += [(outer_from, outer_ref), (inner_from, inner_ref), (skip_from, skip_ref)]
-    moves.append((query_from, query_ref))
+    own = pl.ds(pl.multiple_of(where_ref[1] * CHB, CHB), CHB)
+    moves += [(query_from, query_ref), (cot_from, cot_ref), (weight_from.at[:, own], keep_ref)]
     loads = start_all(moves, sems)
     place = lax.rem(where_ref[0], SPLIT) * OWN
     row = lax.broadcasted_iota(jnp.int32, (OWN, PANEL), 0)
@@ -161,12 +168,16 @@
                 spot = (lane + (a + b) * PANEL).astype(F32)
                 taps = chosen[:, b * PANEL : (b + 1) * PANEL] * jnp.exp(-rate * spot)
                 mid_ref[0, pl.ds((a + b) * PITCH, OWN), :] = taps
-    wait_all(loads[1 + SPLIT :])
+    wait_all(loads[1 + SPLIT : -2])
     own_skip_ref[...] = own_column(skip_ref)
     for c in range(0, CHB, CHUNK):
         at = pl.ds(c, CHUNK)
         turned_ref[at, :] = query_ref[:, at].astype(F32).T.astype(BF16)
-    writes = []
+    wait_all(loads[-2:])
+    for c in range(0, CHB, CHUNK):
+        at = pl.ds(c, CHUNK)
+        share_ref[at, :] = dot_rows(keep_ref[at, :], cot_ref[...])
+    writes = start_all([(share_ref, share_to)], sems, len(moves))
 
     def store(c, rows):
         part = pl.ds(c * TURNS, 4 * TURNS)
@@ -187,7 +198,7 @@
     cot1_ref,
     cot2_ref,
     cot3_ref,
-    cot0_ref,
+    share_from,
     filter_from,
     outer_back_from,
     inner_back_from,
@@ -200,6 +211,7 @@
     inner_back_ref,
     filter_ref,
     cot_ref,
+    share_ref,
     weight_ref,
     sems,
 ):
@@ -208,17 +220,25 @@
         (inner_back_from, inner_back_ref),
         (filter_from, filter_ref),
     ]
-    moves += [(ref, cot_ref.at[s]) for s, ref in enumerate((cot0_ref, cot1_ref, cot2_ref, cot3_ref))]
+    moves += [(ref, cot_ref.at[s]) for s, ref in enumerate((cot1_ref, cot2_ref, cot3_ref))]
+    moves.append((share_from, share_ref))
     loads = start_all(moves, sems)
 
-    def weight_copy(n):
+    def weight_copies(n):
         rows = pl.ds(pl.multiple_of(n * CHUNK, CHUNK), CHUNK)
-        return pltpu.make_async_copy(
-            weight_from.at[rows, :], weight_ref.at[rows, :], sems.at[len(moves) + n]
-        )
+        copies = []
+        for s in range(1, SPLIT):
+            block = lax.rem(where_ref[1] + SPLIT - s, SPLIT) * CHB
+            columns = pl.ds(pl.multiple_of(block, CHB), CHB)
+            sem = sems.at[len(moves) + (SPLIT - 1) * n + s - 1]
+            copies.append(
+                pltpu.make_async_copy(weight_from.at[rows, columns], weight_ref.at[s - 1, rows, :], sem)
+            )
+        return copies
 
     for n in range(CHB // CHUNK):
-        weight_copy(n).start()
+        for copy in weight_copies(n):
+            copy.start()
     for a in range(PANELS):
         mid_ref[0, pl.ds(a * PITCH, OWN), :] = x_ref[a].astype(F32)
 
@@ -247,16 +267,14 @@
 
     gather_panels(mid_ref, inner_back_ref[...], 1, store_panel)
     wait_all(loads[3:])
-    starts = [lax.rem(where_ref[1] + SPLIT - s, SPLIT) * CHB for s in range(SPLIT)]
-    columns = [pl.ds(pl.multiple_of(start, CHB), CHB) for start in starts]
 
     @pl.loop(0, CHB // CHUNK)
     def _(n):
-        weight_copy(n).wait()
+        wait_all(weight_copies(n))
         at = pl.ds(pl.multiple_of(n * CHUNK, CHUNK), CHUNK)
-        total = dot_rows(weight_ref[at, columns[0]], cot_ref[0])
-        for s in range(1, SPLIT):
-            total += dot_rows(weight_ref[at, columns[s]], cot_ref[s])
+        total = share_ref[at, :]
+        for s in range(SPLIT - 1):
+            total += dot_rows(weight_ref[s, at, :], cot_ref[s])
         back_ref[at, :] = total
         grad = (query_ref[at, :].astype(F32) * total).astype(BF16)
         for b in range(CHUNK // OWN):
@@ -481,32 +499,37 @@
     return call(product_kernel, [HBM] * 2, out, scratch, 1 << 20, "product")(key_in, value_in)
 
 
-def make_filter(where, filter_raw, decay, skip, outer, inner, query):
+def make_filter(where, filter_raw, decay, skip, outer, inner, query, cot, weight):
     out = [far(FREQ, BF16), here((OWN, PANEL), F32), here((OWN, PANEL), F32)]
     out += [here(m.shape, BF16) for m in (outer, inner)] + [here((CHB, PANEL), BF16)]
+    out.append(far((CHB, PANEL), F32))
     scratch = [
         pltpu.VMEM(FREQ, BF16),
         pltpu.VMEM((PANELS * PANEL, PANEL), BF16),
         pltpu.VMEM(decay.shape, F32),
         pltpu.VMEM(skip.shape, F32),
         pltpu.VMEM(BLOCK, BF16),
+        pltpu.VMEM(BLOCK, BF16),
+        pltpu.VMEM((CHB, CHB), BF16),
+        pltpu.VMEM((CHB, PANEL), F32),
         MID,
-        sems(5 + SPLIT + OWN // 4),
+        sems(8 + SPLIT + OWN // 4),
     ]
-    specs = [SMEM] + [HBM] * 6
-    return call(filter_kernel, specs, out, scratch, 1 << 32, "taps", [HBM] + [VMEM] * 5)(
-        where, filter_raw, decay, skip, outer, inner, query
-    )
-
-
-def make_forward(where, x, own_skip, held, query, weight, cots, freq_filter, back_mats):
+    specs = [SMEM] + [HBM] * 8
+    return call(filter_kernel, specs, out, scratch, 1 << 32, "taps", [HBM] + [VMEM] * 5 + [HBM])(
+        where, filter_raw, decay, skip, outer, inner, query, cot, weight
+    )
+
+
+def make_forward(where, x, own_skip, held, query, share, weight, cots, freq_filter, back_mats):
     out = [shape(SENT, BF16), here(FREQ, BF16), here((CHB, PANEL), F32)]
     scratch = [MID] + [pltpu.VMEM(m.shape, BF16) for m in back_mats]
-    scratch += [pltpu.VMEM(FREQ, BF16), pltpu.VMEM((SPLIT, *BLOCK), BF16)]
-    scratch += [pltpu.VMEM(weight.shape, BF16), sems(3 + SPLIT + CHB // CHUNK)]
+    scratch += [pltpu.VMEM(FREQ, BF16), pltpu.VMEM((SPLIT - 1, *BLOCK), BF16)]
+    scratch += [pltpu.VMEM((CHB, PANEL), F32), pltpu.VMEM((SPLIT - 1, CHB, CHB), BF16)]
+    scratch.append(sems(4 + (SPLIT - 1) * (1 + CHB // CHUNK)))
     specs = [SMEM] + [VMEM] * 5 + [ANY] * 3 + [HBM] * 5
     return call(forward_kernel, specs, out, scratch, 1 << 33, "forward")(
-        where, x, own_skip, *held, query, *cots[1:], cots[0], freq_filter, *back_mats, weight
+        where, x, own_skip, *held, query, *cots, share, freq_filter, *back_mats, weight
     )
 
 
@@ -546,13 +569,14 @@
     mats = [jnp.asarray(m) for m in tables()]
     where = jnp.stack([lax.axis_index("ctx"), lax.axis_index("ch")]).astype(jnp.int32)
     lines = (CHB // PANEL, PANEL)
-    cots = [cotangent] + [shifted(cotangent, s) for s in (1, 2, 3)]
+    cots = [shifted(cotangent, s) for s in (1, 2, 3)]
     x = exchange(make_product(key_in, value_in))
-    freq_filter, rate, own_skip, *held, turned = make_filter(
-        where, filter_raw, decay.reshape(lines), skip.reshape(lines), *mats[:2], query
+    lined = (decay.reshape(lines), skip.reshape(lines))
+    freq_filter, rate, own_skip, *held, turned, share = make_filter(
+        where, filter_raw, *lined, *mats[:2], query, cotangent, out_weight
     )
     send, freq_x, back = make_forward(
-        where, x, own_skip, held, turned, out_weight, cots, freq_filter, mats[2:]
+        where, x, own_skip, held, turned, share, out_weight, cots, freq_filter, mats[2:]
     )
     got = exchange(send)
     own, one, two, three, last, d_query = make_middle(

time: 77 us -> 76.5 us (level)
  waiting for transfers between devices: 16 us -> 15 us
    ppermute x6, waiting for transfers between devices: 7.58 us -> 6.58 us  [shifted(): lax.ppermute(value, 'ch', [(i, (i + step) % SPLIT) for i in range(SPLIT)])]
  transfers between devices with their start and end apart: 8 -> 8, of which waited for: 4 -> 5; matrix products, arithmetic and copies ran while one was open for 0% -> 0% of each run, Pallas kernels for 10% -> 11%
where the time goes in v3:
time: 76.5 us; the launch traced here: 76 us
  starting transfers between devices  23.2 us (30%)
  Pallas kernels  22 us (29%)
  blocking collectives  15.1 us (20%)
  waiting for transfers between devices  15 us (20%)
    pallas_call x6, Pallas kernels, bound(): run(*(placed(arg, spec) for arg, spec in zip(args, in_specs, strict=True)))  22 us
    all_to_all x1, blocking collectives, exchange(): return lax.all_to_all(value, 'ctx', 0, 0)  15.1 us
    all_to_all x2, starting transfers between devices, exchange(): return lax.all_to_all(value, 'ctx', 0, 0)  14.5 us
    ppermute x6, starting transfers between devices, shifted(): lax.ppermute(value, 'ch', [(i, (i + step) % SPLIT) for i in range(SPLIT)])  8.69 us
    all_to_all x2, waiting for transfers between devices, exchange(): return lax.all_to_all(value, 'ctx', 0, 0)  8.44 us
    ppermute x6, waiting for transfers between devices, shifted(): lax.ppermute(value, 'ch', [(i, (i + step) % SPLIT) for i in range(SPLIT)])  6.58 us
  transfers between devices with their start and end apart: 8, of which 5 were waited for; matrix products, arithmetic and copies ran while one was open for 0% of the time, Pallas kernels for 11%

profile of v3, /device:TPU:1, one launch (start us, length us, event | category | flops | bytes accessed | tf_op | source)
XLA Modules:
  0.0 76.0 jit_solution(17868051900880841656)
XLA Ops:
  0.6 2.1 %collective-permute-start = (bf16[128,1024]{1,0:T(8,128)(2,1)}, bf16[128,1024]{1,0:T(8,128)(2,1)S(1)}, u32[]{:S(2)}, u32[]{:S(2)}) collective-permute-start(bf16[128,1024]{1,0:T(8,128)(2,1)} %cot_from.1), channel_id=1, source_target_pairs={{0,1},{1,2},{2,3},{3,0},{4,5},{5,6},{6,7},{7,4},{8,9},{9,10},{10,1... | collective-permute-start | bytes 786440 | tf_op jit(solution)/shard_map/ppermute | solution.py:561
  2.7 1.4 %collective-permute-start.2 = (bf16[128,1024]{1,0:T(8,128)(2,1)}, bf16[128,1024]{1,0:T(8,128)(2,1)S(1)}, u32[]{:S(2)}, u32[]{:S(2)}) collective-permute-start(bf16[128,1024]{1,0:T(8,128)(2,1)} %cot_from.1), channel_id=1, source_target_pairs={{0,3},{1,0},{2,1},{3,2},{4,7},{5,4},{6,5},{7,6},{8,11},{9,8},{10,9... | collective-permute-start | bytes 786440 | tf_op jit(solution)/shard_map/ppermute | solution.py:561
  4.1 1.6 %collective-permute-start.1 = (bf16[128,1024]{1,0:T(8,128)(2,1)}, bf16[128,1024]{1,0:T(8,128)(2,1)S(1)}, u32[]{:S(2)}, u32[]{:S(2)}) collective-permute-start(bf16[128,1024]{1,0:T(8,128)(2,1)} %cot_from.1), channel_id=1, source_target_pairs={{0,2},{1,3},{2,0},{3,1},{4,6},{5,7},{6,4},{7,5},{8,10},{9,11},{10,... | collective-permute-start | bytes 786440 | tf_op jit(solution)/shard_map/ppermute | solution.py:561
  5.7 1.9 %product.1 = bf16[32,32,128]{2,1,0:T(8,128)(2,1)} custom-call(bf16[128,1024]{1,0:T(8,128)(2,1)} %key_ref.1, bf16[128,1024]{1,0:T(8,128)(2,1)} %value_ref.1), custom_call_target="tpu_custom_call" | custom-call | flops 1048576 | bytes 1048576 | tf_op jit(solution)/shard_map/product/pallas_call | solution.py:487
  7.6 9.6 %all-to-all-start = ((bf16[32,32,128]{2,1,0:T(8,128)(2,1)}), bf16[32,32,128]{2,1,0:T(8,128)(2,1)S(1)}, u32[]{:S(2)}, u32[]{:S(2)}) async-start(bf16[32,32,128]{2,1,0:T(8,128)(2,1)} %product.1), calls=%async_computation | async-start | bytes 524288 | tf_op jit(solution)/shard_map/all_to_all | solution.py:565
  17.3 0.1 pad_add_fusion.where_ref
  17.3 5.0 %taps.1 = (bf16[2048,256]{1,0:T(8,128)(2,1)}, f32[32,128]{1,0:T(8,128)S(1)}, f32[32,128]{1,0:T(8,128)S(1)}, bf16[128,32]{1,0:T(8,128)(2,1)S(1)}, bf16[256,256]{1...) custom-call(s32[2]{0:T(128)S(1)} %pad_add_fusion.where_ref, bf16[4096,1024]{1,0:T(8,128)(2,1)} %raw_from.1, ...), custom_call_target="tpu_custom_call" | custom-call | flops 4294967296 | bytes 1048576 | tf_op jit(solution)/shard_map/taps/pallas_call | solution.py:487
  22.3 3.8 %all-to-all-done.x_ref = bf16[32,32,128]{2,1,0:T(8,128)(2,1)S(1)} async-done(((bf16[32,32,128]{2,1,0:T(8,128)(2,1)}), bf16[32,32,128]{2,1,0:T(8,128)(2,1)S(1)}, u32[]{:S(2)}, u32[]{:S(2)}) %all-to-all-start) | async-done | bytes 262176 | tf_op jit(solution)/shard_map/all_to_all | solution.py:565
  26.2 0.0 collective-permute-done.cot1_ref
  26.2 0.0 collective-permute-done.2.cot3_ref
  26.2 0.0 collective-permute-done.1.cot2_ref
  26.2 5.3 %forward.1 = (bf16[32,64,128]{2,1,0:T(8,128)(2,1)S(1)}, bf16[2048,256]{1,0:T(8,128)(2,1)S(1)}, f32[1024,128]{1,0:T(8,128)S(1)}) custom-call(s32[2]{0:T(128)S(1)} %pad_add_fusion.where_ref, bf16[32,32,128]{2,1,0:T(8,128)(2,1)S(1)} %all-to-all-done.x_ref, f32[32,128]{1,0:T(8,128)S(1)} %get-tuple-element.26.own_skip_ref, ...), custom_call_target="tpu_custom_call" | custom-call | flops 8589934592 | bytes 1048576 | tf_op jit(solution)/shard_map/forward/pallas_call | solution.py:487
  31.5 15.1 %all_to_all.15.got_ref = bf16[32,64,128]{2,1,0:T(8,128)(2,1)S(1)} all-to-all(bf16[32,64,128]{2,1,0:T(8,128)(2,1)S(1)} %get-tuple-element.32), channel_id=1, replica_groups=mesh['ctx'=32,'ch'=4] {'ctx'}, dimensions={0} | all-to-all | bytes 1048576 | tf_op jit(solution)/shard_map/all_to_all | solution.py:565
  46.6 6.8 %middle.1 = (bf16[128,1024]{1,0:T(8,128)(2,1)}, bf16[128,1024]{1,0:T(8,128)(2,1)}, bf16[128,1024]{1,0:T(8,128)(2,1)}, bf16[128,1024]{1,0:T(8,128)(2,1)}, bf16[32...) custom-call(s32[2]{0:T(128)S(1)} %pad_add_fusion.where_ref, bf16[32,64,128]{2,1,0:T(8,128)(2,1)S(1)} %all_to_all.15.got_ref, ...), custom_call_target="tpu_custom_call" | custom-call | flops 8589934592 | bytes 1048576 | tf_op jit(solution)/shard_map/middle/pallas_call | solution.py:487
  53.4 0.4 collective-permute-start.3
  53.8 1.7 %collective-permute-start.4 = (bf16[128,1024]{1,0:T(8,128)(2,1)}, bf16[128,1024]{1,0:T(8,128)(2,1)S(1)}, u32[]{:S(2)}, u32[]{:S(2)}) collective-permute-start(bf16[128,1024]{1,0:T(8,128)(2,1)} %get-tuple-element.38), channel_id=1, source_target_pairs={{0,2},{1,3},{2,0},{3,1},{4,6},{5,7},{6,4},{7,5},{8,10},{9,11},{10,... | collective-permute-start | bytes 786440 | tf_op jit(solution)/shard_map/ppermute | solution.py:561
  55.5 1.5 %collective-permute-start.5 = (bf16[128,1024]{1,0:T(8,128)(2,1)}, bf16[128,1024]{1,0:T(8,128)(2,1)S(1)}, u32[]{:S(2)}, u32[]{:S(2)}) collective-permute-start(bf16[128,1024]{1,0:T(8,128)(2,1)} %get-tuple-element.39), channel_id=1, source_target_pairs={{0,3},{1,0},{2,1},{3,2},{4,7},{5,4},{6,5},{7,6},{8,11},{9,8},{10,9... | collective-permute-start | bytes 786440 | tf_op jit(solution)/shard_map/ppermute | solution.py:561
  57.0 4.8 %all-to-all-start.2 = ((bf16[32,80,128]{2,1,0:T(8,128)(2,1)}), bf16[32,80,128]{2,1,0:T(8,128)(2,1)S(1)}, u32[]{:S(2)}, u32[]{:S(2)}) async-start(bf16[32,80,128]{2,1,0:T(8,128)(2,1)} %get-tuple-element.41), calls=%async_computation.2 | async-start | bytes 1310720 | tf_op jit(solution)/shard_map/all_to_all | solution.py:565
  61.8 1.1 %collective-permute-done.3.one_ref = bf16[128,1024]{1,0:T(8,128)(2,1)S(1)} collective-permute-done((bf16[128,1024]{1,0:T(8,128)(2,1)}, bf16[128,1024]{1,0:T(8,128)(2,1)S(1)}, u32[]{:S(2)}, u32[]{:S(2)}) %collective-permute-start.3) | collective-permute-done | bytes 262176 | tf_op jit(solution)/shard_map/ppermute | solution.py:561
  63.0 4.4 %collective-permute-done.4.two_ref = bf16[128,1024]{1,0:T(8,128)(2,1)S(1)} collective-permute-done((bf16[128,1024]{1,0:T(8,128)(2,1)}, bf16[128,1024]{1,0:T(8,128)(2,1)S(1)}, u32[]{:S(2)}, u32[]{:S(2)}) %collective-permute-start.4) | collective-permute-done | bytes 262176 | tf_op jit(solution)/shard_map/ppermute | solution.py:561
  67.4 1.0 %collective-permute-done.5.three_ref = bf16[128,1024]{1,0:T(8,128)(2,1)S(1)} collective-permute-done((bf16[128,1024]{1,0:T(8,128)(2,1)}, bf16[128,1024]{1,0:T(8,128)(2,1)S(1)}, u32[]{:S(2)}, u32[]{:S(2)}) %collective-permute-start.5) | collective-permute-done | bytes 262176 | tf_op jit(solution)/shard_map/ppermute | solution.py:561
  68.4 1.9 %mixed.1 = bf16[128,1024]{1,0:T(8,128)(2,1)} custom-call(bf16[128,1024]{1,0:T(8,128)(2,1)} %get-tuple-element.36.own_from, bf16[128,1024]{1,0:T(8,128)(2,1)S(1)} %collective-permute-done.3.one_ref, bf16[128,1024]{1,0:T(8,128)(2,1)S(1)} %collective-permute-done.4.two_ref, bf16[128,1024]{1,0:T(8,128)(2,1)S(1)} %collective-permute-done.5.three_ref), custom_call_target="tpu_custom_call" | custom-call | flops 68719476736 | bytes 1048576 | tf_op jit(solution)/shard_map/mixed/pallas_call | solution.py:487
  70.3 4.6 %all-to-all-done.2.got_ref = bf16[32,80,128]{2,1,0:T(8,128)(2,1)S(1)} async-done(((bf16[32,80,128]{2,1,0:T(8,128)(2,1)}), bf16[32,80,128]{2,1,0:T(8,128)(2,1)S(1)}, u32[]{:S(2)}, u32[]{:S(2)}) %all-to-all-start.2) | async-done | bytes 655392 | tf_op jit(solution)/shard_map/all_to_all | solution.py:565
  74.9 1.2 %finish.1 = (bf16[128,1024]{1,0:T(8,128)(2,1)}, bf16[128,1024]{1,0:T(8,128)(2,1)}, f32[128,1024]{1,0:T(8,128)}, f32[8,128]{1,0:T(8,128)}) custom-call(bf16[32,80,128]{2,1,0:T(8,128)(2,1)S(1)} %all-to-all-done.2.got_ref, bf16[128,1024]{1,0:T(8,128)(2,1)S(1)} %copy-done, bf16[128,1024]{1,0:T(8,128)(2,1)S(1)} %copy-done.1), custom_call_target="tpu_custom_call" | custom-call | flops 1048576 | bytes 1048576 | tf_op jit(solution)/shard_map/finish/pallas_call | solution.py:487
  (4 shorter events, 0.0 us)
Async XLA Ops:
  0.6 25.5 %collective-permute-start = (bf16[128,1024]{1,0:T(8,128)(2,1)}, bf16[128,1024]{1,0:T(8,128)(2,1)S(1)}, u32[]{:S(2)}, u32[]{:S(2)}) collective-permute-start(bf16[128,1024]{1,0:T(8,128)(2,1)} %cot_from.1), channel_id=1, source_target_pairs={{0,1},{1,2},{2,3},{3,0},{4,5},{5,6},{6,7},{7,4},{8,9},{9,10},{10,1... | collective-permute-start | bytes 786440 | tf_op jit(solution)/shard_map/ppermute | solution.py:561
  2.7 23.4 %collective-permute-start.2 = (bf16[128,1024]{1,0:T(8,128)(2,1)}, bf16[128,1024]{1,0:T(8,128)(2,1)S(1)}, u32[]{:S(2)}, u32[]{:S(2)}) collective-permute-start(bf16[128,1024]{1,0:T(8,128)(2,1)} %cot_from.1), channel_id=1, source_target_pairs={{0,3},{1,0},{2,1},{3,2},{4,7},{5,4},{6,5},{7,6},{8,11},{9,8},{10,9... | collective-permute-start | bytes 786440 | tf_op jit(solution)/shard_map/ppermute | solution.py:561
  4.1 22.1 %collective-permute-start.1 = (bf16[128,1024]{1,0:T(8,128)(2,1)}, bf16[128,1024]{1,0:T(8,128)(2,1)S(1)}, u32[]{:S(2)}, u32[]{:S(2)}) collective-permute-start(bf16[128,1024]{1,0:T(8,128)(2,1)} %cot_from.1), channel_id=1, source_target_pairs={{0,2},{1,3},{2,0},{3,1},{4,6},{5,7},{6,4},{7,5},{8,10},{9,11},{10,... | collective-permute-start | bytes 786440 | tf_op jit(solution)/shard_map/ppermute | solution.py:561
  7.6 18.5 %all-to-all-start = ((bf16[32,32,128]{2,1,0:T(8,128)(2,1)}), bf16[32,32,128]{2,1,0:T(8,128)(2,1)S(1)}, u32[]{:S(2)}, u32[]{:S(2)}) async-start(bf16[32,32,128]{2,1,0:T(8,128)(2,1)} %product.1), calls=%async_computation | async-start | bytes 524288 | tf_op jit(solution)/shard_map/all_to_all | solution.py:565
  53.4 9.5 %collective-permute-start.3 = (bf16[128,1024]{1,0:T(8,128)(2,1)}, bf16[128,1024]{1,0:T(8,128)(2,1)S(1)}, u32[]{:S(2)}, u32[]{:S(2)}) collective-permute-start(bf16[128,1024]{1,0:T(8,128)(2,1)} %get-tuple-element.37), channel_id=1, source_target_pairs={{0,1},{1,2},{2,3},{3,0},{4,5},{5,6},{6,7},{7,4},{8,9},{9,10},{10,1... | collective-permute-start | bytes 786440 | tf_op jit(solution)/shard_map/ppermute | solution.py:561
  53.8 13.6 %collective-permute-start.4 = (bf16[128,1024]{1,0:T(8,128)(2,1)}, bf16[128,1024]{1,0:T(8,128)(2,1)S(1)}, u32[]{:S(2)}, u32[]{:S(2)}) collective-permute-start(bf16[128,1024]{1,0:T(8,128)(2,1)} %get-tuple-element.38), channel_id=1, source_target_pairs={{0,2},{1,3},{2,0},{3,1},{4,6},{5,7},{6,4},{7,5},{8,10},{9,11},{10,... | collective-permute-start | bytes 786440 | tf_op jit(solution)/shard_map/ppermute | solution.py:561
  55.5 12.9 %collective-permute-start.5 = (bf16[128,1024]{1,0:T(8,128)(2,1)}, bf16[128,1024]{1,0:T(8,128)(2,1)S(1)}, u32[]{:S(2)}, u32[]{:S(2)}) collective-permute-start(bf16[128,1024]{1,0:T(8,128)(2,1)} %get-tuple-element.39), channel_id=1, source_target_pairs={{0,3},{1,0},{2,1},{3,2},{4,7},{5,4},{6,5},{7,6},{8,11},{9,8},{10,9... | collective-permute-start | bytes 786440 | tf_op jit(solution)/shard_map/ppermute | solution.py:561
  57.0 17.9 %all-to-all-start.2 = ((bf16[32,80,128]{2,1,0:T(8,128)(2,1)}), bf16[32,80,128]{2,1,0:T(8,128)(2,1)S(1)}, u32[]{:S(2)}, u32[]{:S(2)}) async-start(bf16[32,80,128]{2,1,0:T(8,128)(2,1)} %get-tuple-element.41), calls=%async_computation.2 | async-start | bytes 1310720 | tf_op jit(solution)/shard_map/all_to_all | solution.py:565
  68.4 6.5 %copy-start = (bf16[128,1024]{1,0:T(8,128)(2,1)S(1)}, bf16[128,1024]{1,0:T(8,128)(2,1)}, u32[]{:S(2)}) copy-start(bf16[128,1024]{1,0:T(8,128)(2,1)} %key_ref.1) | copy-start | bytes 786436
  68.4 6.5 %copy-start.1 = (bf16[128,1024]{1,0:T(8,128)(2,1)S(1)}, bf16[128,1024]{1,0:T(8,128)(2,1)}, u32[]{:S(2)}) copy-start(bf16[128,1024]{1,0:T(8,128)(2,1)} %value_ref.1) | copy-start | bytes 786436

commit v4 on v3

--- a/solution.py
+++ b/solution.py
@@ -413,18 +413,28 @@
     wait_all(writes)
 
 
-def mixed_kernel(own_from, one_ref, two_ref, three_ref, mixed_ref, own_ref, sem):
-    copy = pltpu.make_async_copy(own_from, own_ref, sem)
-    copy.start()
-    copy.wait()
+def pair_kernel(own_from, two_ref, pair_ref, own_ref, sem):
+    load = pltpu.make_async_copy(own_from, own_ref, sem)
+    load.start()
+    load.wait()
     for c in range(0, CHB, CHUNK):
         at = pl.ds(c, CHUNK)
-        mixed = own_ref[:, at].astype(F32) + one_ref[:, at].astype(F32)
-        mixed += two_ref[:, at].astype(F32) + three_ref[:, at].astype(F32)
-        mixed_ref[:, at] = mixed.astype(BF16)
-
-
-def finish_kernel(got_ref, key_ref, value_ref, d_key_ref, d_value_ref, lag_ref, skip_grad_ref):
+        pair_ref[:, at] = own_ref[:, at].astype(F32) + two_ref[:, at].astype(F32)
+
+
+def finish_kernel(
+    got_ref,
+    key_ref,
+    value_ref,
+    pair_ref,
+    one_ref,
+    three_ref,
+    mixed_ref,
+    d_key_ref,
+    d_value_ref,
+    lag_ref,
+    skip_grad_ref,
+):
     for c in range(0, CHB, CHUNK):
         at = pl.ds(c, CHUNK)
         block = pl.ds(c // OWN, CHUNK // OWN)
@@ -432,6 +442,8 @@
         grad = got_ref[block, :OWN, :].reshape(CHUNK, PANEL).astype(F32).T
         d_key_ref[:, at] = (grad * value_ref[:, at].astype(F32)).astype(BF16)
         d_value_ref[:, at] = (grad * key_ref[:, at].astype(F32)).astype(BF16)
+        both = one_ref[:, at].astype(F32) + three_ref[:, at].astype(F32)
+        mixed_ref[:, at] = (pair_ref[:, at] + both).astype(BF16)
     for r in range(PANELS // SPLIT):
         line = jnp.zeros((1, PANEL), F32)
         for b in range(SPLIT):
@@ -546,15 +558,16 @@
     )
 
 
-def make_mixed(parts):
+def make_pair(own, two):
     scratch = [pltpu.VMEM(BLOCK, BF16), pltpu.SemaphoreType.DMA]
-    specs = [HBM] + [VMEM] * 3
-    return call(mixed_kernel, specs, shape(BLOCK, BF16), scratch, 1 << 36, "mixed")(*parts)
-
-
-def make_finish(got, key_in, value_in):
-    out = [shape(BLOCK, BF16)] * 2 + [shape(BLOCK, F32), shape((CHB // PANEL, PANEL), F32)]
-    return call(finish_kernel, [VMEM] * 3, out, [], 1 << 20, "finish")(got, key_in, value_in)
+    return call(pair_kernel, [HBM, VMEM], here(BLOCK, F32), scratch, 1 << 36, "pair")(own, two)
+
+
+def make_finish(got, key_in, value_in, pair, one, three):
+    out = [shape(BLOCK, BF16)] * 3 + [shape(BLOCK, F32), shape((CHB // PANEL, PANEL), F32)]
+    return call(finish_kernel, [VMEM] * 6, out, [], 1 << 20, "finish")(
+        got, key_in, value_in, pair, one, three
+    )
 
 
 def shifted(value, step):
@@ -583,8 +596,10 @@
         where, got, x, freq_x, rate, own_skip, held, turned, back, freq_filter, *mats[2:], out_weight
     )
     last = exchange(last)
-    mixed = make_mixed([own, shifted(one, 1), shifted(two, 2), shifted(three, 3)])
-    d_key, d_value, filter_grad, skip_grad = make_finish(last, key_in, value_in)
+    pair = make_pair(own, shifted(two, 2))
+    mixed, d_key, d_value, filter_grad, skip_grad = make_finish(
+        last, key_in, value_in, pair, shifted(one, 1), shifted(three, 3)
+    )
     return (mixed, d_query, d_key, d_value, filter_grad, skip_grad.reshape(CHB))
 
 

time: 76.5 us -> 73.9 us (0.966)
  waiting for transfers between devices: 15 us -> 13 us
    all_to_all x2, waiting for transfers between devices: 8.44 us -> 7.44 us  [exchange(): return lax.all_to_all(value, 'ctx', 0, 0)]
    ppermute x6, waiting for transfers between devices: 6.58 us -> 5.61 us  [shifted(): lax.ppermute(value, 'ch', [(i, (i + step) % SPLIT) for i in range(SPLIT)])]
  transfers between devices with their start and end apart: 8 -> 8, of which waited for: 5 -> 4; matrix products, arithmetic and copies ran while one was open for 0% -> 0% of each run, Pallas kernels for 11% -> 11%
where the time goes in v4:
time: 73.9 us; the launch traced here: 73.5 us
  starting transfers between devices  23.3 us (32%)
  Pallas kernels  21.3 us (29%)
  blocking collectives  15.1 us (20%)
  waiting for transfers between devices  13 us (18%)
    pallas_call x6, Pallas kernels, bound(): run(*(placed(arg, spec) for arg, spec in zip(args, in_specs, strict=True)))  21.3 us
    all_to_all x1, blocking collectives, exchange(): return lax.all_to_all(value, 'ctx', 0, 0)  15.1 us
    all_to_all x2, starting transfers between devices, exchange(): return lax.all_to_all(value, 'ctx', 0, 0)  13.9 us
    ppermute x6, starting transfers between devices, shifted(): lax.ppermute(value, 'ch', [(i, (i + step) % SPLIT) for i in range(SPLIT)])  9.37 us
    all_to_all x2, waiting for transfers between devices, exchange(): return lax.all_to_all(value, 'ctx', 0, 0)  7.44 us
    ppermute x6, waiting for transfers between devices, shifted(): lax.ppermute(value, 'ch', [(i, (i + step) % SPLIT) for i in range(SPLIT)])  5.61 us
  transfers between devices with their start and end apart: 8, of which 4 were waited for; matrix products, arithmetic and copies ran while one was open for 0% of the time, Pallas kernels for 11%

profile of v4, /device:TPU:1, one launch (start us, length us, event | category | flops | bytes accessed | tf_op | source)
XLA Modules:
  0.0 73.5 jit_solution(6758415534388584463)
XLA Ops:
  0.6 2.1 %collective-permute-start = (bf16[128,1024]{1,0:T(8,128)(2,1)}, bf16[128,1024]{1,0:T(8,128)(2,1)S(1)}, u32[]{:S(2)}, u32[]{:S(2)}) collective-permute-start(bf16[128,1024]{1,0:T(8,128)(2,1)} %cot_from.1), channel_id=1, source_target_pairs={{0,1},{1,2},{2,3},{3,0},{4,5},{5,6},{6,7},{7,4},{8,9},{9,10},{10,1... | collective-permute-start | bytes 786440 | tf_op jit(solution)/shard_map/ppermute | solution.py:574
  2.7 1.4 %collective-permute-start.2 = (bf16[128,1024]{1,0:T(8,128)(2,1)}, bf16[128,1024]{1,0:T(8,128)(2,1)S(1)}, u32[]{:S(2)}, u32[]{:S(2)}) collective-permute-start(bf16[128,1024]{1,0:T(8,128)(2,1)} %cot_from.1), channel_id=1, source_target_pairs={{0,3},{1,0},{2,1},{3,2},{4,7},{5,4},{6,5},{7,6},{8,11},{9,8},{10,9... | collective-permute-start | bytes 786440 | tf_op jit(solution)/shard_map/ppermute | solution.py:574
  4.1 1.6 %collective-permute-start.1 = (bf16[128,1024]{1,0:T(8,128)(2,1)}, bf16[128,1024]{1,0:T(8,128)(2,1)S(1)}, u32[]{:S(2)}, u32[]{:S(2)}) collective-permute-start(bf16[128,1024]{1,0:T(8,128)(2,1)} %cot_from.1), channel_id=1, source_target_pairs={{0,2},{1,3},{2,0},{3,1},{4,6},{5,7},{6,4},{7,5},{8,10},{9,11},{10,... | collective-permute-start | bytes 786440 | tf_op jit(solution)/shard_map/ppermute | solution.py:574
  5.7 1.9 %product.1 = bf16[32,32,128]{2,1,0:T(8,128)(2,1)} custom-call(bf16[128,1024]{1,0:T(8,128)(2,1)} %key_ref.1, bf16[128,1024]{1,0:T(8,128)(2,1)} %value_ref.1), custom_call_target="tpu_custom_call" | custom-call | flops 1048576 | bytes 1048576 | tf_op jit(solution)/shard_map/product/pallas_call | solution.py:499
  7.6 9.6 %all-to-all-start = ((bf16[32,32,128]{2,1,0:T(8,128)(2,1)}), bf16[32,32,128]{2,1,0:T(8,128)(2,1)S(1)}, u32[]{:S(2)}, u32[]{:S(2)}) async-start(bf16[32,32,128]{2,1,0:T(8,128)(2,1)} %product.1), calls=%async_computation | async-start | bytes 524288 | tf_op jit(solution)/shard_map/all_to_all | solution.py:578
  17.3 0.1 pad_add_fusion.where_ref
  17.3 5.0 %taps.1 = (bf16[2048,256]{1,0:T(8,128)(2,1)}, f32[32,128]{1,0:T(8,128)S(1)}, f32[32,128]{1,0:T(8,128)S(1)}, bf16[128,32]{1,0:T(8,128)(2,1)S(1)}, bf16[256,256]{1...) custom-call(s32[2]{0:T(128)S(1)} %pad_add_fusion.where_ref, bf16[4096,1024]{1,0:T(8,128)(2,1)} %raw_from.1, ...), custom_call_target="tpu_custom_call" | custom-call | flops 4294967296 | bytes 1048576 | tf_op jit(solution)/shard_map/taps/pallas_call | solution.py:499
  22.3 3.8 %all-to-all-done.x_ref = bf16[32,32,128]{2,1,0:T(8,128)(2,1)S(1)} async-done(((bf16[32,32,128]{2,1,0:T(8,128)(2,1)}), bf16[32,32,128]{2,1,0:T(8,128)(2,1)S(1)}, u32[]{:S(2)}, u32[]{:S(2)}) %all-to-all-start) | async-done | bytes 262176 | tf_op jit(solution)/shard_map/all_to_all | solution.py:578
  26.2 0.0 collective-permute-done.cot1_ref
  26.2 0.0 collective-permute-done.2.cot3_ref
  26.2 0.0 collective-permute-done.1.cot2_ref
  26.2 5.3 %forward.1 = (bf16[32,64,128]{2,1,0:T(8,128)(2,1)S(1)}, bf16[2048,256]{1,0:T(8,128)(2,1)S(1)}, f32[1024,128]{1,0:T(8,128)S(1)}) custom-call(s32[2]{0:T(128)S(1)} %pad_add_fusion.where_ref, bf16[32,32,128]{2,1,0:T(8,128)(2,1)S(1)} %all-to-all-done.x_ref, f32[32,128]{1,0:T(8,128)S(1)} %get-tuple-element.27.own_skip_ref, ...), custom_call_target="tpu_custom_call" | custom-call | flops 8589934592 | bytes 1048576 | tf_op jit(solution)/shard_map/forward/pallas_call | solution.py:499
  31.5 15.1 %all_to_all.15.got_ref = bf16[32,64,128]{2,1,0:T(8,128)(2,1)S(1)} all-to-all(bf16[32,64,128]{2,1,0:T(8,128)(2,1)S(1)} %get-tuple-element.33), channel_id=1, replica_groups=mesh['ctx'=32,'ch'=4] {'ctx'}, dimensions={0} | all-to-all | bytes 1048576 | tf_op jit(solution)/shard_map/all_to_all | solution.py:578
  46.6 6.8 %middle.1 = (bf16[128,1024]{1,0:T(8,128)(2,1)}, bf16[128,1024]{1,0:T(8,128)(2,1)}, bf16[128,1024]{1,0:T(8,128)(2,1)}, bf16[128,1024]{1,0:T(8,128)(2,1)}, bf16[32...) custom-call(s32[2]{0:T(128)S(1)} %pad_add_fusion.where_ref, bf16[32,64,128]{2,1,0:T(8,128)(2,1)S(1)} %all_to_all.15.got_ref, ...), custom_call_target="tpu_custom_call" | custom-call | flops 8589934592 | bytes 1048576 | tf_op jit(solution)/shard_map/middle/pallas_call | solution.py:499
  53.4 1.5 %collective-permute-start.3 = (bf16[128,1024]{1,0:T(8,128)(2,1)}, bf16[128,1024]{1,0:T(8,128)(2,1)S(1)}, u32[]{:S(2)}, u32[]{:S(2)}) collective-permute-start(bf16[128,1024]{1,0:T(8,128)(2,1)} %get-tuple-element.39), channel_id=1, source_target_pairs={{0,2},{1,3},{2,0},{3,1},{4,6},{5,7},{6,4},{7,5},{8,10},{9,11},{10,... | collective-permute-start | bytes 786440 | tf_op jit(solution)/shard_map/ppermute | solution.py:574
  54.9 4.3 %all-to-all-start.2 = ((bf16[32,80,128]{2,1,0:T(8,128)(2,1)}), bf16[32,80,128]{2,1,0:T(8,128)(2,1)S(1)}, u32[]{:S(2)}, u32[]{:S(2)}) async-start(bf16[32,80,128]{2,1,0:T(8,128)(2,1)} %get-tuple-element.37), calls=%async_computation.2 | async-start | bytes 1310720 | tf_op jit(solution)/shard_map/all_to_all | solution.py:578
  59.2 0.1 collective-permute-start.4
  59.3 2.7 %collective-permute-start.5 = (bf16[128,1024]{1,0:T(8,128)(2,1)}, bf16[128,1024]{1,0:T(8,128)(2,1)S(1)}, u32[]{:S(2)}, u32[]{:S(2)}) collective-permute-start(bf16[128,1024]{1,0:T(8,128)(2,1)} %get-tuple-element.41), channel_id=1, source_target_pairs={{0,3},{1,0},{2,1},{3,2},{4,7},{5,4},{6,5},{7,6},{8,11},{9,8},{10,9... | collective-permute-start | bytes 786440 | tf_op jit(solution)/shard_map/ppermute | solution.py:574
  62.0 0.7 collective-permute-done.3.two_ref
  62.6 1.1 %pair.1.pair_ref = f32[128,1024]{1,0:T(8,128)S(1)} custom-call(bf16[128,1024]{1,0:T(8,128)(2,1)} %get-tuple-element.38.own_from, bf16[128,1024]{1,0:T(8,128)(2,1)S(1)} %collective-permute-done.3.two_ref), custom_call_target="tpu_custom_call" | custom-call | flops 68719476736 | bytes 1048576 | tf_op jit(solution)/shard_map/pair/pallas_call | solution.py:499
  63.7 4.9 %collective-permute-done.4.one_ref = bf16[128,1024]{1,0:T(8,128)(2,1)S(1)} collective-permute-done((bf16[128,1024]{1,0:T(8,128)(2,1)}, bf16[128,1024]{1,0:T(8,128)(2,1)S(1)}, u32[]{:S(2)}, u32[]{:S(2)}) %collective-permute-start.4) | collective-permute-done | bytes 262176 | tf_op jit(solution)/shard_map/ppermute | solution.py:574
  68.6 0.0 collective-permute-done.5.three_ref
  68.6 3.6 %all-to-all-done.2.got_ref = bf16[32,80,128]{2,1,0:T(8,128)(2,1)S(1)} async-done(((bf16[32,80,128]{2,1,0:T(8,128)(2,1)}), bf16[32,80,128]{2,1,0:T(8,128)(2,1)S(1)}, u32[]{:S(2)}, u32[]{:S(2)}) %all-to-all-start.2) | async-done | bytes 655392 | tf_op jit(solution)/shard_map/all_to_all | solution.py:578
  72.2 1.3 %finish.1 = (bf16[128,1024]{1,0:T(8,128)(2,1)}, bf16[128,1024]{1,0:T(8,128)(2,1)}, bf16[128,1024]{1,0:T(8,128)(2,1)}, f32[128,1024]{1,0:T(8,128)}, f32[8,128]{1,0:T(8,128)}) custom-call(bf16[32,80,128]{2,1,0:T(8,128)(2,1)S(1)} %all-to-all-done.2.got_ref, bf16[128,1024]{1,0:T(8,128)(2,1)S(1)} %copy-done, bf16[128,1024]{1,0:T(8,128)(2,1)S(1)} %copy-done.1, ...), custom_call_target="tpu_custom_call" | custom-call | flops 1048576 | bytes 1048576 | tf_op jit(solution)/shard_map/finish/pallas_call | solution.py:499
  (4 shorter events, 0.0 us)
Async XLA Ops:
  0.6 25.5 %collective-permute-start = (bf16[128,1024]{1,0:T(8,128)(2,1)}, bf16[128,1024]{1,0:T(8,128)(2,1)S(1)}, u32[]{:S(2)}, u32[]{:S(2)}) collective-permute-start(bf16[128,1024]{1,0:T(8,128)(2,1)} %cot_from.1), channel_id=1, source_target_pairs={{0,1},{1,2},{2,3},{3,0},{4,5},{5,6},{6,7},{7,4},{8,9},{9,10},{10,1... | collective-permute-start | bytes 786440 | tf_op jit(solution)/shard_map/ppermute | solution.py:574
  2.7 23.4 %collective-permute-start.2 = (bf16[128,1024]{1,0:T(8,128)(2,1)}, bf16[128,1024]{1,0:T(8,128)(2,1)S(1)}, u32[]{:S(2)}, u32[]{:S(2)}) collective-permute-start(bf16[128,1024]{1,0:T(8,128)(2,1)} %cot_from.1), channel_id=1, source_target_pairs={{0,3},{1,0},{2,1},{3,2},{4,7},{5,4},{6,5},{7,6},{8,11},{9,8},{10,9... | collective-permute-start | bytes 786440 | tf_op jit(solution)/shard_map/ppermute | solution.py:574
  4.1 22.1 %collective-permute-start.1 = (bf16[128,1024]{1,0:T(8,128)(2,1)}, bf16[128,1024]{1,0:T(8,128)(2,1)S(1)}, u32[]{:S(2)}, u32[]{:S(2)}) collective-permute-start(bf16[128,1024]{1,0:T(8,128)(2,1)} %cot_from.1), channel_id=1, source_target_pairs={{0,2},{1,3},{2,0},{3,1},{4,6},{5,7},{6,4},{7,5},{8,10},{9,11},{10,... | collective-permute-start | bytes 786440 | tf_op jit(solution)/shard_map/ppermute | solution.py:574
  7.6 18.5 %all-to-all-start = ((bf16[32,32,128]{2,1,0:T(8,128)(2,1)}), bf16[32,32,128]{2,1,0:T(8,128)(2,1)S(1)}, u32[]{:S(2)}, u32[]{:S(2)}) async-start(bf16[32,32,128]{2,1,0:T(8,128)(2,1)} %product.1), calls=%async_computation | async-start | bytes 524288 | tf_op jit(solution)/shard_map/all_to_all | solution.py:578
  53.4 9.2 %collective-permute-start.3 = (bf16[128,1024]{1,0:T(8,128)(2,1)}, bf16[128,1024]{1,0:T(8,128)(2,1)S(1)}, u32[]{:S(2)}, u32[]{:S(2)}) collective-permute-start(bf16[128,1024]{1,0:T(8,128)(2,1)} %get-tuple-element.39), channel_id=1, source_target_pairs={{0,2},{1,3},{2,0},{3,1},{4,6},{5,7},{6,4},{7,5},{8,10},{9,11},{10,... | collective-permute-start | bytes 786440 | tf_op jit(solution)/shard_map/ppermute | solution.py:574
  54.9 17.3 %all-to-all-start.2 = ((bf16[32,80,128]{2,1,0:T(8,128)(2,1)}), bf16[32,80,128]{2,1,0:T(8,128)(2,1)S(1)}, u32[]{:S(2)}, u32[]{:S(2)}) async-start(bf16[32,80,128]{2,1,0:T(8,128)(2,1)} %get-tuple-element.37), calls=%async_computation.2 | async-start | bytes 1310720 | tf_op jit(solution)/shard_map/all_to_all | solution.py:578
  59.2 9.4 %collective-permute-start.4 = (bf16[128,1024]{1,0:T(8,128)(2,1)}, bf16[128,1024]{1,0:T(8,128)(2,1)S(1)}, u32[]{:S(2)}, u32[]{:S(2)}) collective-permute-start(bf16[128,1024]{1,0:T(8,128)(2,1)} %get-tuple-element.40), channel_id=1, source_target_pairs={{0,1},{1,2},{2,3},{3,0},{4,5},{5,6},{6,7},{7,4},{8,9},{9,10},{10,1... | collective-permute-start | bytes 786440 | tf_op jit(solution)/shard_map/ppermute | solution.py:574
  59.3 9.3 %collective-permute-start.5 = (bf16[128,1024]{1,0:T(8,128)(2,1)}, bf16[128,1024]{1,0:T(8,128)(2,1)S(1)}, u32[]{:S(2)}, u32[]{:S(2)}) collective-permute-start(bf16[128,1024]{1,0:T(8,128)(2,1)} %get-tuple-element.41), channel_id=1, source_target_pairs={{0,3},{1,0},{2,1},{3,2},{4,7},{5,4},{6,5},{7,6},{8,11},{9,8},{10,9... | collective-permute-start | bytes 786440 | tf_op jit(solution)/shard_map/ppermute | solution.py:574
  62.6 9.6 %copy-start = (bf16[128,1024]{1,0:T(8,128)(2,1)S(1)}, bf16[128,1024]{1,0:T(8,128)(2,1)}, u32[]{:S(2)}) copy-start(bf16[128,1024]{1,0:T(8,128)(2,1)} %key_ref.1) | copy-start | bytes 786436
  62.6 9.6 %copy-start.1 = (bf16[128,1024]{1,0:T(8,128)(2,1)S(1)}, bf16[128,1024]{1,0:T(8,128)(2,1)}, u32[]{:S(2)}) copy-start(bf16[128,1024]{1,0:T(8,128)(2,1)} %value_ref.1) | copy-start | bytes 786436

commit v5 on v4

--- a/solution.py
+++ b/solution.py
@@ -429,12 +429,18 @@
     pair_ref,
     one_ref,
     three_ref,
+    mixed_to,
+    d_key_to,
+    d_value_to,
+    lag_to,
+    skip_grad_ref,
     mixed_ref,
     d_key_ref,
     d_value_ref,
     lag_ref,
-    skip_grad_ref,
+    sems,
 ):
+    writes = []
     for c in range(0, CHB, CHUNK):
         at = pl.ds(c, CHUNK)
         block = pl.ds(c // OWN, CHUNK // OWN)
@@ -444,12 +450,16 @@
         d_value_ref[:, at] = (grad * key_ref[:, at].astype(F32)).astype(BF16)
         both = one_ref[:, at].astype(F32) + three_ref[:, at].astype(F32)
         mixed_ref[:, at] = (pair_ref[:, at] + both).astype(BF16)
+        outs = ((lag_ref, lag_to), (d_key_ref, d_key_to), (d_value_ref, d_value_to), (mixed_ref, mixed_to))
+        moves = [(this.at[:, at], to.at[:, at]) for this, to in outs]
+        writes += start_all(moves, sems, len(writes))
     for r in range(PANELS // SPLIT):
         line = jnp.zeros((1, PANEL), F32)
         for b in range(SPLIT):
             tail = got_ref[r * SPLIT + b, 2 * OWN :, :].astype(F32)
             line += tail[0:1] + tail[1:2]
         skip_grad_ref[pl.ds(r, 1), :] = line
+    wait_all(writes)
 
 
 VMEM = pl.BlockSpec(memory_space=pltpu.VMEM)
@@ -565,7 +575,9 @@
 
 def make_finish(got, key_in, value_in, pair, one, three):
     out = [shape(BLOCK, BF16)] * 3 + [shape(BLOCK, F32), shape((CHB // PANEL, PANEL), F32)]
-    return call(finish_kernel, [VMEM] * 6, out, [], 1 << 20, "finish")(
+    scratch = [pltpu.VMEM(BLOCK, BF16)] * 3 + [pltpu.VMEM(BLOCK, F32), sems(4 * CHB // CHUNK)]
+    specs = [HBM] * 4 + [VMEM]
+    return call(finish_kernel, [VMEM] * 6, out, scratch, 1 << 20, "finish", specs)(
         got, key_in, value_in, pair, one, three
     )
 

time: 73.9 us -> 74.5 us (level)
  no operation moved by 1% of the time
where the time goes in v5:
time: 74.5 us; the launch traced here: 74.1 us
  starting transfers between devices  23.3 us (31%)
  Pallas kernels  21.9 us (29%)
  blocking collectives  15.1 us (20%)
  waiting for transfers between devices  13 us (17%)
    pallas_call x6, Pallas kernels, bound(): run(*(placed(arg, spec) for arg, spec in zip(args, in_specs, strict=True)))  21.9 us
    all_to_all x1, blocking collectives, exchange(): return lax.all_to_all(value, 'ctx', 0, 0)  15.1 us
    all_to_all x2, starting transfers between devices, exchange(): return lax.all_to_all(value, 'ctx', 0, 0)  13.9 us
    ppermute x6, starting transfers between devices, shifted(): lax.ppermute(value, 'ch', [(i, (i + step) % SPLIT) for i in range(SPLIT)])  9.37 us
    all_to_all x2, waiting for transfers between devices, exchange(): return lax.all_to_all(value, 'ctx', 0, 0)  7.44 us
    ppermute x6, waiting for transfers between devices, shifted(): lax.ppermute(value, 'ch', [(i, (i + step) % SPLIT) for i in range(SPLIT)])  5.61 us
  transfers between devices with their start and end apart: 8, of which 4 were waited for; matrix products, arithmetic and copies ran while one was open for 0% of the time, Pallas kernels for 11%

profile of v5, /device:TPU:1, one launch (start us, length us, event | category | flops | bytes accessed | tf_op | source)
XLA Modules:
  0.0 74.1 jit_solution(12329688154459727977)
XLA Ops:
  0.6 2.1 %collective-permute-start = (bf16[128,1024]{1,0:T(8,128)(2,1)}, bf16[128,1024]{1,0:T(8,128)(2,1)S(1)}, u32[]{:S(2)}, u32[]{:S(2)}) collective-permute-start(bf16[128,1024]{1,0:T(8,128)(2,1)} %cot_from.1), channel_id=1, source_target_pairs={{0,1},{1,2},{2,3},{3,0},{4,5},{5,6},{6,7},{7,4},{8,9},{9,10},{10,1... | collective-permute-start | bytes 786440 | tf_op jit(solution)/shard_map/ppermute | solution.py:586
  2.7 1.4 %collective-permute-start.2 = (bf16[128,1024]{1,0:T(8,128)(2,1)}, bf16[128,1024]{1,0:T(8,128)(2,1)S(1)}, u32[]{:S(2)}, u32[]{:S(2)}) collective-permute-start(bf16[128,1024]{1,0:T(8,128)(2,1)} %cot_from.1), channel_id=1, source_target_pairs={{0,3},{1,0},{2,1},{3,2},{4,7},{5,4},{6,5},{7,6},{8,11},{9,8},{10,9... | collective-permute-start | bytes 786440 | tf_op jit(solution)/shard_map/ppermute | solution.py:586
  4.1 1.6 %collective-permute-start.1 = (bf16[128,1024]{1,0:T(8,128)(2,1)}, bf16[128,1024]{1,0:T(8,128)(2,1)S(1)}, u32[]{:S(2)}, u32[]{:S(2)}) collective-permute-start(bf16[128,1024]{1,0:T(8,128)(2,1)} %cot_from.1), channel_id=1, source_target_pairs={{0,2},{1,3},{2,0},{3,1},{4,6},{5,7},{6,4},{7,5},{8,10},{9,11},{10,... | collective-permute-start | bytes 786440 | tf_op jit(solution)/shard_map/ppermute | solution.py:586
  5.7 1.9 %product.1 = bf16[32,32,128]{2,1,0:T(8,128)(2,1)} custom-call(bf16[128,1024]{1,0:T(8,128)(2,1)} %key_ref.1, bf16[128,1024]{1,0:T(8,128)(2,1)} %value_ref.1), custom_call_target="tpu_custom_call" | custom-call | flops 1048576 | bytes 1048576 | tf_op jit(solution)/shard_map/product/pallas_call | solution.py:509
  7.6 9.6 %all-to-all-start = ((bf16[32,32,128]{2,1,0:T(8,128)(2,1)}), bf16[32,32,128]{2,1,0:T(8,128)(2,1)S(1)}, u32[]{:S(2)}, u32[]{:S(2)}) async-start(bf16[32,32,128]{2,1,0:T(8,128)(2,1)} %product.1), calls=%async_computation | async-start | bytes 524288 | tf_op jit(solution)/shard_map/all_to_all | solution.py:590
  17.3 0.1 pad_add_fusion.where_ref
  17.3 5.0 %taps.1 = (bf16[2048,256]{1,0:T(8,128)(2,1)}, f32[32,128]{1,0:T(8,128)S(1)}, f32[32,128]{1,0:T(8,128)S(1)}, bf16[128,32]{1,0:T(8,128)(2,1)S(1)}, bf16[256,256]{1...) custom-call(s32[2]{0:T(128)S(1)} %pad_add_fusion.where_ref, bf16[4096,1024]{1,0:T(8,128)(2,1)} %raw_from.1, ...), custom_call_target="tpu_custom_call" | custom-call | flops 4294967296 | bytes 1048576 | tf_op jit(solution)/shard_map/taps/pallas_call | solution.py:509
  22.3 3.8 %all-to-all-done.x_ref = bf16[32,32,128]{2,1,0:T(8,128)(2,1)S(1)} async-done(((bf16[32,32,128]{2,1,0:T(8,128)(2,1)}), bf16[32,32,128]{2,1,0:T(8,128)(2,1)S(1)}, u32[]{:S(2)}, u32[]{:S(2)}) %all-to-all-start) | async-done | bytes 262176 | tf_op jit(solution)/shard_map/all_to_all | solution.py:590
  26.2 0.0 collective-permute-done.cot1_ref
  26.2 0.0 collective-permute-done.2.cot3_ref
  26.2 0.0 collective-permute-done.1.cot2_ref
  26.2 5.3 %forward.1 = (bf16[32,64,128]{2,1,0:T(8,128)(2,1)S(1)}, bf16[2048,256]{1,0:T(8,128)(2,1)S(1)}, f32[1024,128]{1,0:T(8,128)S(1)}) custom-call(s32[2]{0:T(128)S(1)} %pad_add_fusion.where_ref, bf16[32,32,128]{2,1,0:T(8,128)(2,1)S(1)} %all-to-all-done.x_ref, f32[32,128]{1,0:T(8,128)S(1)} %get-tuple-element.27.own_skip_ref, ...), custom_call_target="tpu_custom_call" | custom-call | flops 8589934592 | bytes 1048576 | tf_op jit(solution)/shard_map/forward/pallas_call | solution.py:509
  31.5 15.1 %all_to_all.15.got_ref = bf16[32,64,128]{2,1,0:T(8,128)(2,1)S(1)} all-to-all(bf16[32,64,128]{2,1,0:T(8,128)(2,1)S(1)} %get-tuple-element.33), channel_id=1, replica_groups=mesh['ctx'=32,'ch'=4] {'ctx'}, dimensions={0} | all-to-all | bytes 1048576 | tf_op jit(solution)/shard_map/all_to_all | solution.py:590
  46.6 6.8 %middle.1 = (bf16[128,1024]{1,0:T(8,128)(2,1)}, bf16[128,1024]{1,0:T(8,128)(2,1)}, bf16[128,1024]{1,0:T(8,128)(2,1)}, bf16[128,1024]{1,0:T(8,128)(2,1)}, bf16[32...) custom-call(s32[2]{0:T(128)S(1)} %pad_add_fusion.where_ref, bf16[32,64,128]{2,1,0:T(8,128)(2,1)S(1)} %all_to_all.15.got_ref, ...), custom_call_target="tpu_custom_call" | custom-call | flops 8589934592 | bytes 1048576 | tf_op jit(solution)/shard_map/middle/pallas_call | solution.py:509
  53.4 1.5 %collective-permute-start.3 = (bf16[128,1024]{1,0:T(8,128)(2,1)}, bf16[128,1024]{1,0:T(8,128)(2,1)S(1)}, u32[]{:S(2)}, u32[]{:S(2)}) collective-permute-start(bf16[128,1024]{1,0:T(8,128)(2,1)} %get-tuple-element.39), channel_id=1, source_target_pairs={{0,2},{1,3},{2,0},{3,1},{4,6},{5,7},{6,4},{7,5},{8,10},{9,11},{10,... | collective-permute-start | bytes 786440 | tf_op jit(solution)/shard_map/ppermute | solution.py:586
  54.9 4.3 %all-to-all-start.2 = ((bf16[32,80,128]{2,1,0:T(8,128)(2,1)}), bf16[32,80,128]{2,1,0:T(8,128)(2,1)S(1)}, u32[]{:S(2)}, u32[]{:S(2)}) async-start(bf16[32,80,128]{2,1,0:T(8,128)(2,1)} %get-tuple-element.37), calls=%async_computation.2 | async-start | bytes 1310720 | tf_op jit(solution)/shard_map/all_to_all | solution.py:590
  59.2 0.1 collective-permute-start.4
  59.3 2.7 %collective-permute-start.5 = (bf16[128,1024]{1,0:T(8,128)(2,1)}, bf16[128,1024]{1,0:T(8,128)(2,1)S(1)}, u32[]{:S(2)}, u32[]{:S(2)}) collective-permute-start(bf16[128,1024]{1,0:T(8,128)(2,1)} %get-tuple-element.41), channel_id=1, source_target_pairs={{0,3},{1,0},{2,1},{3,2},{4,7},{5,4},{6,5},{7,6},{8,11},{9,8},{10,9... | collective-permute-start | bytes 786440 | tf_op jit(solution)/shard_map/ppermute | solution.py:586
  62.0 0.7 collective-permute-done.3.two_ref
  62.6 1.1 %pair.1.pair_ref = f32[128,1024]{1,0:T(8,128)S(1)} custom-call(bf16[128,1024]{1,0:T(8,128)(2,1)} %get-tuple-element.38.own_from, bf16[128,1024]{1,0:T(8,128)(2,1)S(1)} %collective-permute-done.3.two_ref), custom_call_target="tpu_custom_call" | custom-call | flops 68719476736 | bytes 1048576 | tf_op jit(solution)/shard_map/pair/pallas_call | solution.py:509
  63.7 4.9 %collective-permute-done.4.one_ref = bf16[128,1024]{1,0:T(8,128)(2,1)S(1)} collective-permute-done((bf16[128,1024]{1,0:T(8,128)(2,1)}, bf16[128,1024]{1,0:T(8,128)(2,1)S(1)}, u32[]{:S(2)}, u32[]{:S(2)}) %collective-permute-start.4) | collective-permute-done | bytes 262176 | tf_op jit(solution)/shard_map/ppermute | solution.py:586
  68.6 0.0 collective-permute-done.5.three_ref
  68.6 3.6 %all-to-all-done.2.got_ref = bf16[32,80,128]{2,1,0:T(8,128)(2,1)S(1)} async-done(((bf16[32,80,128]{2,1,0:T(8,128)(2,1)}), bf16[32,80,128]{2,1,0:T(8,128)(2,1)S(1)}, u32[]{:S(2)}, u32[]{:S(2)}) %all-to-all-start.2) | async-done | bytes 655392 | tf_op jit(solution)/shard_map/all_to_all | solution.py:590
  72.2 1.9 %finish.1 = (bf16[128,1024]{1,0:T(8,128)(2,1)}, bf16[128,1024]{1,0:T(8,128)(2,1)}, bf16[128,1024]{1,0:T(8,128)(2,1)}, f32[128,1024]{1,0:T(8,128)}, f32[8,128]{1,0:T(8,128)}) custom-call(bf16[32,80,128]{2,1,0:T(8,128)(2,1)S(1)} %all-to-all-done.2.got_ref, bf16[128,1024]{1,0:T(8,128)(2,1)S(1)} %copy-done, bf16[128,1024]{1,0:T(8,128)(2,1)S(1)} %copy-done.1, ...), custom_call_target="tpu_custom_call" | custom-call | flops 1048576 | bytes 1048576 | tf_op jit(solution)/shard_map/finish/pallas_call | solution.py:509
  (4 shorter events, 0.0 us)
Async XLA Ops:
  0.6 25.5 %collective-permute-start = (bf16[128,1024]{1,0:T(8,128)(2,1)}, bf16[128,1024]{1,0:T(8,128)(2,1)S(1)}, u32[]{:S(2)}, u32[]{:S(2)}) collective-permute-start(bf16[128,1024]{1,0:T(8,128)(2,1)} %cot_from.1), channel_id=1, source_target_pairs={{0,1},{1,2},{2,3},{3,0},{4,5},{5,6},{6,7},{7,4},{8,9},{9,10},{10,1... | collective-permute-start | bytes 786440 | tf_op jit(solution)/shard_map/ppermute | solution.py:586
  2.7 23.4 %collective-permute-start.2 = (bf16[128,1024]{1,0:T(8,128)(2,1)}, bf16[128,1024]{1,0:T(8,128)(2,1)S(1)}, u32[]{:S(2)}, u32[]{:S(2)}) collective-permute-start(bf16[128,1024]{1,0:T(8,128)(2,1)} %cot_from.1), channel_id=1, source_target_pairs={{0,3},{1,0},{2,1},{3,2},{4,7},{5,4},{6,5},{7,6},{8,11},{9,8},{10,9... | collective-permute-start | bytes 786440 | tf_op jit(solution)/shard_map/ppermute | solution.py:586
  4.1 22.1 %collective-permute-start.1 = (bf16[128,1024]{1,0:T(8,128)(2,1)}, bf16[128,1024]{1,0:T(8,128)(2,1)S(1)}, u32[]{:S(2)}, u32[]{:S(2)}) collective-permute-start(bf16[128,1024]{1,0:T(8,128)(2,1)} %cot_from.1), channel_id=1, source_target_pairs={{0,2},{1,3},{2,0},{3,1},{4,6},{5,7},{6,4},{7,5},{8,10},{9,11},{10,... | collective-permute-start | bytes 786440 | tf_op jit(solution)/shard_map/ppermute | solution.py:586
  7.6 18.5 %all-to-all-start = ((bf16[32,32,128]{2,1,0:T(8,128)(2,1)}), bf16[32,32,128]{2,1,0:T(8,128)(2,1)S(1)}, u32[]{:S(2)}, u32[]{:S(2)}) async-start(bf16[32,32,128]{2,1,0:T(8,128)(2,1)} %product.1), calls=%async_computation | async-start | bytes 524288 | tf_op jit(solution)/shard_map/all_to_all | solution.py:590
  53.4 9.2 %collective-permute-start.3 = (bf16[128,1024]{1,0:T(8,128)(2,1)}, bf16[128,1024]{1,0:T(8,128)(2,1)S(1)}, u32[]{:S(2)}, u32[]{:S(2)}) collective-permute-start(bf16[128,1024]{1,0:T(8,128)(2,1)} %get-tuple-element.39), channel_id=1, source_target_pairs={{0,2},{1,3},{2,0},{3,1},{4,6},{5,7},{6,4},{7,5},{8,10},{9,11},{10,... | collective-permute-start | bytes 786440 | tf_op jit(solution)/shard_map/ppermute | solution.py:586
  54.9 17.3 %all-to-all-start.2 = ((bf16[32,80,128]{2,1,0:T(8,128)(2,1)}), bf16[32,80,128]{2,1,0:T(8,128)(2,1)S(1)}, u32[]{:S(2)}, u32[]{:S(2)}) async-start(bf16[32,80,128]{2,1,0:T(8,128)(2,1)} %get-tuple-element.37), calls=%async_computation.2 | async-start | bytes 1310720 | tf_op jit(solution)/shard_map/all_to_all | solution.py:590
  59.2 9.4 %collective-permute-start.4 = (bf16[128,1024]{1,0:T(8,128)(2,1)}, bf16[128,1024]{1,0:T(8,128)(2,1)S(1)}, u32[]{:S(2)}, u32[]{:S(2)}) collective-permute-start(bf16[128,1024]{1,0:T(8,128)(2,1)} %get-tuple-element.40), channel_id=1, source_target_pairs={{0,1},{1,2},{2,3},{3,0},{4,5},{5,6},{6,7},{7,4},{8,9},{9,10},{10,1... | collective-permute-start | bytes 786440 | tf_op jit(solution)/shard_map/ppermute | solution.py:586
  59.3 9.3 %collective-permute-start.5 = (bf16[128,1024]{1,0:T(8,128)(2,1)}, bf16[128,1024]{1,0:T(8,128)(2,1)S(1)}, u32[]{:S(2)}, u32[]{:S(2)}) collective-permute-start(bf16[128,1024]{1,0:T(8,128)(2,1)} %get-tuple-element.41), channel_id=1, source_target_pairs={{0,3},{1,0},{2,1},{3,2},{4,7},{5,4},{6,5},{7,6},{8,11},{9,8},{10,9... | collective-permute-start | bytes 786440 | tf_op jit(solution)/shard_map/ppermute | solution.py:586
  62.6 9.6 %copy-start = (bf16[128,1024]{1,0:T(8,128)(2,1)S(1)}, bf16[128,1024]{1,0:T(8,128)(2,1)}, u32[]{:S(2)}) copy-start(bf16[128,1024]{1,0:T(8,128)(2,1)} %key_ref.1) | copy-start | bytes 786436
  62.6 9.6 %copy-start.1 = (bf16[128,1024]{1,0:T(8,128)(2,1)S(1)}, bf16[128,1024]{1,0:T(8,128)(2,1)}, u32[]{:S(2)}) copy-start(bf16[128,1024]{1,0:T(8,128)(2,1)} %value_ref.1) | copy-start | bytes 786436
